TPU v7x, 768 devices: a whole 4x8x12 slice. The times are simulated.
768 devices in a mesh: gx: 24 (over z, core), gy: 8 (over y), gz: 4 (over x).
Axes of the slice: x: 4, y: 8, z: 12, core: 2. Of those that a mesh axis runs over, the one named last changes fastest.
Arguments:
- operator: bfloat16 [24, 8, 3072, 3072], P('gx', 'gy', 'gz'), may hold values from -1 to 4
- rhs_parts: float32 [24, 8, 8, 3072], P('gx', 'gy'), may hold values from -6 to 6
- stiffness: float32 [24, 8, 3072], P('gx', 'gy'), may hold values from 1 to 10
- traces: float32 [24, 8, 6, 3072], P('gx', 'gy'), may hold values from -6 to 6
- coarse_inverse: float32 [24, 8, 6, 1152], P('gx', 'gy'), may hold values from -1 to 1, as said below
- rigid_loads: float32 [24, 8, 6, 8], P('gx', 'gy'), may hold values from -8192 to 8192
- face_lengths: int32 [24, 8, 4], P('gx', 'gy'), may hold values from 0 to 768, as said below
- face_order: int32 [24, 8, 4, 768], P('gx', 'gy'), may hold values from 0 to 767, as said below
- mode_count: int32 [24, 8], P('gx', 'gy'), may hold values from 0 to 6, as said below
Outputs:
- multipliers: float32 [24, 8, 8, 3072], P('gx', 'gy')
Inputs may be any that keep to these rules, and one draw needn't show every extreme that they name: `coarse_inverse`: symmetric over the coefficient ordering. `face_lengths`: a face on the grid's edge has length 0; the two sides of an interface have the same length. `face_order`: on each face the live slots map one to one onto the neighbour's live slots of the opposite face, and that face maps them back; other slots map to themselves. `mode_count`: subdomains off the grid's edge have 6.
All inputs are finite; a program needn't handle non-finite values.
Results may differ from a plain program's by a relative error of at most 0.0036.
Values may be sent and summed in bfloat16 or wider, within the bound.
A program may use at most 32 MiB of HBM per device.

v0:
```python
import jax
import jax.numpy as jnp
from jax import lax
from jax.sharding import PartitionSpec as P

ITERS = 2


highest = lax.Precision.HIGHEST


def with_halo(block, sides, width):
    for axis, dim in sides:
        count = lax.axis_size(axis)
        forward = [(i, i + 1) for i in range(count - 1)]
        backward = [(target, source) for source, target in forward]
        low = lax.ppermute(
            lax.slice_in_dim(block, block.shape[dim] - width, None, axis=dim), axis, forward
        )
        high = lax.ppermute(lax.slice_in_dim(block, 0, width, axis=dim), axis, backward)
        block = jnp.concatenate([low, block, high], axis=dim)
    return block


def shards(
    operator,
    rhs_parts,
    stiffness,
    traces,
    coarse_inverse,
    rigid_loads,
    face_lengths,
    face_order,
    mode_count,
):
    local_rows = operator[0, 0]
    right_side = rhs_parts[0, 0]
    stiff_local = stiffness[0, 0]
    modes_local = traces[0, 0]
    inverse_rows = coarse_inverse[0, 0]
    loads_modes = rigid_loads[0, 0]
    lengths = face_lengths[0, 0]
    partner_slots = face_order[0, 0]
    modes_live = mode_count[0, 0]
    mode_total, order_size = modes_local.shape
    face_slots = partner_slots.shape[1]
    load_count = right_side.shape[0]
    position = lax.broadcasted_iota(jnp.int32, (4, face_slots), 1)
    live_mask = (position < lengths[:, None]).astype(jnp.float32).reshape(order_size)
    mode_mask = (lax.broadcasted_iota(jnp.int32, (mode_total, 1), 0) < modes_live).astype(
        jnp.float32
    )
    active_modes = modes_local * mode_mask
    face_start = lax.broadcasted_iota(jnp.int32, (4, face_slots), 0) * face_slots
    flat_slots = (partner_slots + face_start).reshape(order_size)

    def partner(vectors):
        row_count = vectors.shape[0]
        blocks = vectors.reshape(row_count, 4, face_slots)
        x_rim = with_halo(jnp.stack([blocks[:, 0], blocks[:, 1]], axis=0), (("gx", 0),), 1)
        y_rim = with_halo(jnp.stack([blocks[:, 2], blocks[:, 3]], axis=0), (("gy", 0),), 1)
        facing = jnp.stack([x_rim[0], x_rim[3], y_rim[0], y_rim[3]], axis=1).reshape(
            row_count, order_size
        )
        return jnp.take(facing, flat_slots, axis=1)

    def assemble(vectors):
        return live_mask * (vectors + partner(vectors))

    def coarse_step(local_coarse, partial_value):
        pieces, partials = (
            lax.all_gather(local_coarse[None], ("gx", "gy"), axis=0, tiled=True),
            lax.all_gather(partial_value[None], ("gx", "gy"), axis=0, tiled=True),
        )
        stacked = pieces.reshape(-1, load_count)
        own_coeffs = jnp.dot(inverse_rows, stacked, precision=highest)
        return (own_coeffs, None, jnp.sum(partials, axis=0))

    def correction(own_coeffs):
        own_term = jnp.einsum("ml,mi->li", own_coeffs, active_modes, precision=highest)
        return assemble(own_term)

    def product_rows(vectors):
        own_part = jnp.einsum(
            "lj,ij->li",
            vectors.astype(jnp.bfloat16),
            local_rows,
            preferred_element_type=jnp.float32,
        )
        return own_part.astype(jnp.bfloat16)

    def assembled_product(vectors, subtract_from):
        own_rows = product_rows(vectors)
        full_rows = lax.all_gather(own_rows, "gz", axis=1, tiled=True).astype(jnp.float32)
        if subtract_from is None:
            return assemble(full_rows)
        return assemble(subtract_from - full_rows)

    nothing = jnp.zeros((load_count,), jnp.float32)
    start_coeffs, start_grid, discard = coarse_step(mode_mask * loads_modes, nothing)
    start_term = jnp.einsum("ml,mi->li", start_coeffs, active_modes, precision=highest)
    outgoing = [start_term, stiff_local[None]] + []
    received = partner(jnp.concatenate(outgoing, axis=0))
    estimate = live_mask * (start_term + received[:load_count])
    weight = live_mask / (live_mask * (stiff_local + received[load_count]) + 1.0 - live_mask)

    def project(vectors, partial_value, needed):
        local_coarse = jnp.einsum("mi,li->ml", active_modes, vectors, precision=highest)
        own_coeffs, coarse_grid, dot_total = coarse_step(local_coarse, partial_value)
        if needed:
            return (vectors - correction(own_coeffs), dot_total)
        return (vectors, dot_total)

    gap = assembled_product(estimate, right_side)
    residual, discard = project(gap, nothing, True)
    direction = residual
    previous = nothing
    for iteration in range(ITERS):
        scaled = weight * residual
        projected, resid_dot = project(scaled, jnp.sum(residual * scaled, axis=1), True)
        if iteration == 0:
            direction = projected
        else:
            direction = projected + (resid_dot / previous)[:, None] * direction
        image = assembled_product(direction, None)
        corrected, curvature = project(
            image, jnp.sum(direction * image, axis=1), iteration + 1 < ITERS
        )
        step_size = resid_dot / curvature
        estimate = estimate + step_size[:, None] * direction
        if iteration + 1 < ITERS:
            residual = residual - step_size[:, None] * corrected
        previous = resid_dot
    return estimate[None, None]


def solution(mesh):
    in_specs = (
        P("gx", "gy", "gz", None),
        P("gx", "gy", None, None),
        P("gx", "gy", None),
        P("gx", "gy", None, None),
        P("gx", "gy", None, None),
        P("gx", "gy", None, None),
        P("gx", "gy", None),
        P("gx", "gy", None, None),
        P("gx", "gy"),
    )
    out_specs = P("gx", "gy", None, None)
    return jax.shard_map(shards, mesh=mesh, in_specs=in_specs, out_specs=out_specs, check_vma=False)
```

profile of v0, /device:TPU:1, one launch (start us, length us, event | category | flops | bytes accessed | tf_op | source)
XLA Modules:
  0.0 2312.1 jit_solution(7983284101908831723)
XLA Ops:
  1.5 125.4 %all_gather.36 = f32[192,6,8]{2,1,0:T(8,128)S(1)} all-gather(f32[1,6,8]{2,1,0:T(8,128)S(1)} %copy.49), channel_id=1, replica_groups=mesh['gx'=24,'gy'=8,'gz'=4] {'gx','gy'}, dimensions={0}, use_global_device_ids=true | all-gather | bytes 37056 | tf_op jit(solution)/shard_map/all_gather | solution.py:72
  141.4 8.1 gather_fusion
  154.1 9.4 all_gather.37
  168.8 5.3 collective-permute-start.5
  179.7 9.6 gather_fusion.1
  191.0 111.8 %all-gather.8 = f32[192,6,8]{2,1,0:T(8,128)S(1)} all-gather(f32[1,6,8]{2,1,0:T(8,128)S(1)} %convolution_bitcast_fusion.3), channel_id=2, replica_groups=mesh['gx'=24,'gy'=8,'gz'=4] {'gx','gy'}, dimensions={0}, use_global_device_ids=true | all-gather | bytes 37056 | tf_op jit(solution)/shard_map/all_gather | solution.py:72
  317.1 9.6 gather_fusion.2
  330.0 115.3 %all-gather.9 = f32[192,6,8]{2,1,0:T(8,128)S(1)} all-gather(f32[1,6,8]{2,1,0:T(8,128)S(1)} %convolution_bitcast_fusion.2), channel_id=4, replica_groups=mesh['gx'=24,'gy'=8,'gz'=4] {'gx','gy'}, dimensions={0}, use_global_device_ids=true | all-gather | bytes 37056 | tf_op jit(solution)/shard_map/all_gather | solution.py:72
  448.1 5.2 collective-permute-start.14
  460.3 8.1 gather_fusion.3
  473.2 9.2 all_gather.41
  487.7 5.2 collective-permute-start.17
  500.1 8.1 gather_fusion.4
  509.4 118.4 %all-gather.10 = f32[192,6,8]{2,1,0:T(8,128)S(1)} all-gather(f32[1,6,8]{2,1,0:T(8,128)S(1)} %convolution_bitcast_fusion.1), channel_id=6, replica_groups=mesh['gx'=24,'gy'=8,'gz'=4] {'gx','gy'}, dimensions={0}, use_global_device_ids=true | all-gather | bytes 37056 | tf_op jit(solution)/shard_map/all_gather | solution.py:72
  630.5 4.7 collective-permute-start.22
  641.3 728.4 %all-reduce.4 = (f32[1536]{0:T(1024)S(1)}, f32[1536]{0:T(1024)S(1)}) all-reduce(f32[1536]{0:T(1024)S(1)} %dynamic-update-slice, f32[1536]{0:T(1024)S(1)} %dynamic-update-slice.1), channel_id=3, replica_groups=mesh['gx'=24,'gy'=8,'gz'=4] {'gx','gy'}, use_global_device_ids=true, to_apply=%add | all-reduce | flops 3072 | bytes 24576
  1371.0 9.6 gather_fusion.5
  1383.4 122.9 %all-gather.11 = f32[192,6,8]{2,1,0:T(8,128)S(1)} all-gather(f32[1,6,8]{2,1,0:T(8,128)S(1)} %convolution_bitcast_fusion), channel_id=8, replica_groups=mesh['gx'=24,'gy'=8,'gz'=4] {'gx','gy'}, dimensions={0}, use_global_device_ids=true | all-gather | bytes 37056 | tf_op jit(solution)/shard_map/all_gather | solution.py:72
  1519.0 367.3 %all-reduce.2 = f32[1536]{0:T(1024)S(1)} all-reduce(f32[1536]{0:T(1024)S(1)} %dynamic-update-slice.2), channel_id=7, replica_groups=mesh['gx'=24,'gy'=8,'gz'=4] {'gx','gy'}, use_global_device_ids=true, to_apply=%add.2 | all-reduce | flops 1536 | bytes 12288
  1887.6 8.1 gather_fusion.6
  1900.6 9.2 all_gather.46
  1915.1 14.4 collective-permute-start.29
  1933.1 8.1 gather_fusion.7
  1942.1 369.0 %all-reduce.3 = f32[1536]{0:T(1024)S(1)} all-reduce(f32[1536]{0:T(1024)S(1)} %dynamic-update-slice.3), channel_id=9, replica_groups=mesh['gx'=24,'gy'=8,'gz'=4] {'gx','gy'}, use_global_device_ids=true, to_apply=%add.3 | all-reduce | flops 1536 | bytes 12288
  (254 shorter events, 119.1 us)
Async XLA Ops:
  128.4 12.4 collective-permute-start.3
  129.7 11.2 collective-permute-start.2
  133.7 7.2 collective-permute-start.1
  163.5 15.6 collective-permute-start.7
  164.8 14.3 collective-permute-start.6
  168.8 10.4 collective-permute-start.5
  304.3 12.0 collective-permute-start.11
  305.6 10.7 collective-permute-start.10
  446.8 12.3 collective-permute-start.15
  448.1 11.0 collective-permute-start.14
  482.4 17.1 collective-permute-start.19
  483.7 15.8 collective-permute-start.18
  487.7 11.8 collective-permute-start.17
  629.2 741.2 %collective-permute-start.23 = (f32[1,8,768]{2,1,0:T(8,128)S(1)}, f32[1,8,768]{2,1,0:T(8,128)S(1)}, u32[]{:S(2)}, u32[]{:S(2)}) collective-permute-start(f32[1,8,768]{2,1,0:T(8,128)S(1)} %get-tuple-element.25), channel_id=1, source_target_pairs={{4,0},{8,4},{12,8},{16,12},{20,16},{24,20},{28,24},{5,1},{9,5},{13... | collective-permute-start | bytes 73736 | tf_op jit(solution)/shard_map/ppermute | solution.py:20
  630.5 739.9 %collective-permute-start.22 = (f32[1,8,768]{2,1,0:T(8,128)S(1)}, f32[1,8,768]{2,1,0:T(8,128)S(1)}, u32[]{:S(2)}, u32[]{:S(2)}) collective-permute-start(f32[1,8,768]{2,1,0:T(8,128)S(1)} %get-tuple-element.26), channel_id=1, source_target_pairs={{0,4},{4,8},{8,12},{12,16},{16,20},{20,24},{24,28},{1,5},{5,9},{9,... | collective-permute-start | bytes 73736 | tf_op jit(solution)/shard_map/ppermute | solution.py:17
  635.3 735.2 %collective-permute-start.21 = (f32[1,8,768]{2,1,0:T(8,128)S(1)}, f32[1,8,768]{2,1,0:T(8,128)S(1)}, u32[]{:S(2)}, u32[]{:S(2)}) collective-permute-start(f32[1,8,768]{2,1,0:T(8,128)S(1)} %get-tuple-element.27), channel_id=1, source_target_pairs={{32,0},{64,32},{96,64},{128,96},{160,128},{192,160},{224,192},{256... | collective-permute-start | bytes 73736 | tf_op jit(solution)/shard_map/ppermute | solution.py:20
  638.4 732.1 %collective-permute-start.20 = (f32[1,8,768]{2,1,0:T(8,128)S(1)}, f32[1,8,768]{2,1,0:T(8,128)S(1)}, u32[]{:S(2)}, u32[]{:S(2)}) collective-permute-start(f32[1,8,768]{2,1,0:T(8,128)S(1)} %get-tuple-element.24), channel_id=1, source_target_pairs={{0,32},{32,64},{64,96},{96,128},{128,160},{160,192},{192,224},{224... | collective-permute-start | bytes 73736 | tf_op jit(solution)/shard_map/ppermute | solution.py:17
  1507.8 379.2 %collective-permute-start.27 = (f32[1,8,768]{2,1,0:T(8,128)S(1)}, f32[1,8,768]{2,1,0:T(8,128)S(1)}, u32[]{:S(2)}, u32[]{:S(2)}) collective-permute-start(f32[1,8,768]{2,1,0:T(8,128)S(1)} %get-tuple-element.21), channel_id=1, source_target_pairs={{4,0},{8,4},{12,8},{16,12},{20,16},{24,20},{28,24},{5,1},{9,5},{13... | collective-permute-start | bytes 73736 | tf_op jit(solution)/shard_map/ppermute | solution.py:20
  1509.1 377.9 %collective-permute-start.26 = (f32[1,8,768]{2,1,0:T(8,128)S(1)}, f32[1,8,768]{2,1,0:T(8,128)S(1)}, u32[]{:S(2)}, u32[]{:S(2)}) collective-permute-start(f32[1,8,768]{2,1,0:T(8,128)S(1)} %get-tuple-element.22), channel_id=1, source_target_pairs={{0,4},{4,8},{8,12},{12,16},{16,20},{20,24},{24,28},{1,5},{5,9},{9,... | collective-permute-start | bytes 73736 | tf_op jit(solution)/shard_map/ppermute | solution.py:17
  1513.1 373.9 %collective-permute-start.25 = (f32[1,8,768]{2,1,0:T(8,128)S(1)}, f32[1,8,768]{2,1,0:T(8,128)S(1)}, u32[]{:S(2)}, u32[]{:S(2)}) collective-permute-start(f32[1,8,768]{2,1,0:T(8,128)S(1)} %get-tuple-element.23), channel_id=1, source_target_pairs={{32,0},{64,32},{96,64},{128,96},{160,128},{192,160},{224,192},{256... | collective-permute-start | bytes 73736 | tf_op jit(solution)/shard_map/ppermute | solution.py:20
  1516.3 370.8 %collective-permute-start.24 = (f32[1,8,768]{2,1,0:T(8,128)S(1)}, f32[1,8,768]{2,1,0:T(8,128)S(1)}, u32[]{:S(2)}, u32[]{:S(2)}) collective-permute-start(f32[1,8,768]{2,1,0:T(8,128)S(1)} %get-tuple-element.20), channel_id=1, source_target_pairs={{0,32},{32,64},{64,96},{96,128},{128,160},{160,192},{192,224},{224... | collective-permute-start | bytes 73736 | tf_op jit(solution)/shard_map/ppermute | solution.py:17
  1909.8 21.7 collective-permute-start.31
  1911.1 20.4 collective-permute-start.30
  1915.1 16.4 collective-permute-start.29
  (54 other events, 4305.1 us)
where the time goes:
time: 2320 us; the launch traced here: 2310 us
  blocking collectives  2090 us (90%)
  starting transfers between devices  108 us (5%)
  local copies, waits for them, and re-layouts  82.2 us (4%)
    unnamed x3, blocking collectives  1460 us
    all_gather x5, blocking collectives, coarse_step(): lax.all_gather(local_coarse[None], ('gx', 'gy'), axis=0, tiled=True)  594 us
    gather x16, local copies, waits for them, and re-layouts, partner(): return jnp.take(facing, flat_slots, axis=1)  72.8 us
    ppermute x16, starting transfers between devices, with_halo(): lax.ppermute(lax.slice_in_dim(block, block.shape[dim] - width, None, axis...  56.9 us
    ppermute x16, starting transfers between devices, with_halo(): lax.ppermute(lax.slice_in_dim(block, 0, width, axis=dim), axis, backward)  50.8 us
  transfers between devices with their start and end apart: 32, of which 3 were waited for; matrix products, arithmetic and copies ran while one was open for 0% of the time, Pallas kernels for 0%

commit v1 on v0

v1 whole, which is shorter than its diff:
```python
import functools

import jax
import jax.numpy as jnp
from jax import lax
from jax.experimental import pallas as pl
from jax.experimental.pallas import tpu as pltpu
from jax.sharding import PartitionSpec as P

MESH = pl.DeviceIdType.MESH
GATHERS = 6
PRODUCTS = 2
LANES = 128


def kernel(
    sizes,
    op_ref,
    rhs_ref,
    stiff_ref,
    traces_ref,
    inverse_ref,
    loads_ref,
    lengths_ref,
    order_ref,
    count_ref,
    out_ref,
    op_v,
    faces_out,
    faces_in,
    rows_pad,
    coarse,
    plane,
    column,
    peers,
    blocks,
    lo_ref,
    hi_ref,
    own_e,
    near_e,
    weight,
    known,
    resid,
    direct,
    image,
    op_sem,
    setup_send,
    setup_recv,
    coarse_send,
    coarse_recv,
    plane_send,
    plane_recv,
    column_send,
    column_recv,
    peer_send,
    peer_recv,
    block_send,
    block_recv,
):
    nx, ny, nz = sizes
    cap = order_ref.shape[1]
    order = rhs_ref.shape[1]
    tiles = cap // LANES
    modes = traces_ref.shape[0]
    chips = nx // 2
    plane_size = 2 * ny
    spread = plane_size * modes
    gx, gy, gz = lax.axis_index("gx"), lax.axis_index("gy"), lax.axis_index("gz")
    chip, core = gx // 2, gx % 2

    def near(face, z):
        sign = 2 * (face % 2) - 1
        along_x = 1 - face // 2
        return (
            lax.rem(gx + along_x * sign + nx, nx),
            lax.rem(gy + (1 - along_x) * sign + ny, ny),
            z,
        )

    def opposite(face):
        return face + 1 - 2 * (face % 2)

    peer_list = [(gx, gy, lax.rem(gz + k, nz)) for k in range(1, nz)]
    plane_list = [
        (chip * 2 + lax.rem(core + c, 2), lax.rem(gy + k, ny), gz)
        for c in range(2)
        for k in range(ny)
        if c or k
    ]
    column_list = [(lax.rem(gx + 2 * k, nx), gy, gz) for k in range(1, chips)]
    face_list = [near(f, gz) for f in range(4)]
    product_list = [near(gz, k) for k in range(nz)]
    source_list = [near(f, opposite(f)) for f in range(4)]

    op_copy = pltpu.make_async_copy(op_ref, op_v, op_sem)
    op_copy.start()

    barrier = pltpu.get_barrier_semaphore()
    greeted = peer_list + plane_list + column_list + face_list + source_list
    for target in greeted:
        pl.semaphore_signal(barrier, inc=1, device_id=target, device_id_type=MESH)

    sub = lax.broadcasted_iota(jnp.int32, (8, LANES), 0)
    lane = lax.broadcasted_iota(jnp.int32, (8, LANES), 1)

    def send(src, dst, send_sem, recv_sem, target):
        pltpu.make_async_remote_copy(
            src_ref=src,
            dst_ref=dst,
            send_sem=send_sem,
            recv_sem=recv_sem,
            device_id=target,
            device_id_type=MESH,
        ).start()

    def await_bytes(ref, sem):
        pltpu.make_async_copy(ref, ref, sem).wait()

    def take(values, index):
        return jnp.take_along_axis(values, index, axis=1, mode="promise_in_bounds")

    def row_of(columns):
        total = jnp.zeros((8, LANES), jnp.float32)
        for m, value in columns:
            total = total + jnp.where(lane == 8 * m + sub, value, 0.0)
        return jnp.sum(total, axis=0, keepdims=True)

    pick = jnp.where(lane < spread, 8 * (lane % modes) + sub, 8 * modes + sub)
    my_slot = core * ny + gy

    def gather_start(g, row):
        plane[g, pl.ds(my_slot, 1), :] = row
        mine = plane.at[g, pl.ds(my_slot, 1)]
        for target in plane_list:
            send(mine, mine, plane_send.at[g], plane_recv.at[g], target)

    def gather_finish(g):
        await_bytes(plane.at[g, pl.ds(0, plane_size - 1)], plane_recv.at[g])
        tile = jnp.zeros((8, LANES), jnp.float32)
        for s in range(plane_size):
            found = take(jnp.broadcast_to(plane[g, s : s + 1, :], (8, LANES)), pick)
            keep = ((lane >= s * modes) & (lane < (s + 1) * modes)) | (lane == spread)
            tile = tile + jnp.where(keep, found, 0.0)
        spot = pl.ds(pl.multiple_of(chip * LANES, LANES), LANES)
        column[g, :, spot] = tile
        mine = column.at[g, :, spot]
        for target in column_list:
            send(mine, mine, column_send.at[g], column_recv.at[g], target)
        await_bytes(column.at[g, :, pl.ds(0, (chips - 1) * LANES)], column_recv.at[g])

    def coefficients(g):
        gathered = column[g]
        return [
            [
                jnp.sum(gathered * coarse[s, m : m + 1, :], axis=1, keepdims=True)
                for m in range(modes)
            ]
            for s in range(5)
        ]

    def dot_total(g):
        gathered = column[g]
        total = gathered[:, :LANES]
        for z in range(1, chips):
            total = total + gathered[:, z * LANES : (z + 1) * LANES]
        return jnp.sum(jnp.where(lane == spread, total, 0.0), axis=1, keepdims=True)

    def face(f):
        return slice(f * cap, (f + 1) * cap)

    def correction(coeffs, f):
        total = jnp.zeros((8, cap), jnp.float32)
        for m in range(modes):
            total = total + coeffs[0][m] * own_e[m : m + 1, face(f)]
            total = total + coeffs[1 + f][m] * near_e[m : m + 1, face(f)]
        return total

    def dots(vector):
        return [
            (m, jnp.sum(vector * own_e[m : m + 1, :], axis=1, keepdims=True))
            for m in range(modes)
        ]

    def dot(a, b):
        return (modes, jnp.sum(a * b, axis=1, keepdims=True))

    def partner_tiles(load, start):
        given = [load(c) for c in range(tiles)]
        for b in range(tiles):
            spot = pl.ds(pl.multiple_of(start + b * LANES, LANES), LANES)
            low, high = lo_ref[:, spot], hi_ref[:, spot]
            result = take(given[0], low)
            for c in range(1, tiles):
                result = jnp.where(high == c, take(given[c], low), result)
            yield b, spot, result

    count = count_ref[0, 0]
    rows_pad[...] = jnp.zeros_like(rows_pad)
    rows_pad[0:modes, 0 : loads_ref.shape[1]] = loads_ref[...]
    loads_tile = jnp.where(sub < count, rows_pad[:, :LANES], 0.0)
    first = jnp.zeros((8, LANES), jnp.float32)
    for m in range(modes):
        only = jnp.where(sub == m, loads_tile, 0.0)
        first = first + (only if m == 0 else pltpu.roll(only, 8 * m, axis=1))
    first = jnp.sum(first, axis=0, keepdims=True)

    live_mode = lax.broadcasted_iota(jnp.int32, (modes, cap), 0) < count
    for f in range(4):
        faces_out[f, 0:modes, :] = jnp.where(live_mode, traces_ref[:, face(f)], 0.0)
        faces_out[f, modes : modes + 1, :] = stiff_ref[:, face(f)]
        faces_out[f, modes + 1 : 8, :] = jnp.zeros((7 - modes, cap), jnp.float32)
        faces_out[f, 8:16, :] = rhs_ref[:, face(f)]
    rows_pad[...] = jnp.zeros_like(rows_pad)
    rows_pad[0:modes, :] = inverse_ref[...]
    for z in range(chips):
        start = z * spread
        base, shift = start // LANES, start % LANES
        chunk = rows_pad[:, base * LANES : (base + 1) * LANES]
        if shift:
            chunk = pltpu.roll(chunk, LANES - shift, axis=1)
            if LANES - shift < spread:
                after = rows_pad[:, (base + 1) * LANES : (base + 2) * LANES]
                after = pltpu.roll(after, LANES - shift, axis=1)
                chunk = jnp.where(lane < LANES - shift, chunk, after)
        coarse[0, :, z * LANES : (z + 1) * LANES] = jnp.where(lane < spread, chunk, 0.0)

    pl.semaphore_wait(barrier, len(greeted))

    gather_start(0, first)
    for f in range(4):
        send(faces_out.at[f], faces_in.at[f + 1 - 2 * (f % 2)], setup_send, setup_recv, face_list[f])
    for f in range(4):
        send(coarse.at[0], coarse.at[2 + f - 2 * (f % 2)], coarse_send, coarse_recv, face_list[f])

    for f in range(4):
        index = jnp.broadcast_to(order_ref[f : f + 1, :], (8, cap))
        lo_ref[:, face(f)] = index & (LANES - 1)
        hi_ref[:, face(f)] = index >> 7

    await_bytes(faces_in, setup_recv)

    def setup_face(f, carry):
        start = pl.multiple_of(f * cap, cap)
        length = lengths_ref[0, f]
        for b, spot, other in partner_tiles(
            lambda c: faces_in[f, 0:8, c * LANES : (c + 1) * LANES], start
        ):
            part = slice(b * LANES, (b + 1) * LANES)
            live = lane + b * LANES < length
            mine = faces_out[f, 0:8, part]
            own_e[:, spot] = jnp.where(live, mine, 0.0)
            near_e[:, spot] = jnp.where(live, other, 0.0)
            stiff = jnp.broadcast_to((mine + other)[modes : modes + 1, :], (8, LANES))
            weight[:, spot] = jnp.where(live, 1.0 / jnp.where(live, stiff, 1.0), 0.0)
        for b, spot, other in partner_tiles(
            lambda c: faces_in[f, 8:16, c * LANES : (c + 1) * LANES], start
        ):
            part = slice(b * LANES, (b + 1) * LANES)
            live = lane + b * LANES < length
            known[:, spot] = jnp.where(live, faces_out[f, 8:16, part] + other, 0.0)
        return carry

    lax.fori_loop(0, 4, setup_face, 0)

    half = cap // 2

    def product(vector):
        return lax.dot_general(
            vector.astype(jnp.bfloat16),
            op_v[...],
            (((1,), (1,)), ((), ())),
            preferred_element_type=jnp.float32,
        )

    def exchange(e, rows):
        packed = jnp.concatenate([rows[:, :half], rows[:, half:]], axis=0)
        blocks[e, gz] = packed.astype(jnp.bfloat16)
        mine = blocks.at[e, gz]
        for target in product_list:
            send(mine, blocks.at[e, 4 + opposite(gz)], block_send.at[e], block_recv.at[e], target)
        for target in peer_list:
            send(mine, mine, block_send.at[e], block_recv.at[e], target)
        await_bytes(blocks.at[e, pl.ds(0, 7)], block_recv.at[e])

        def assemble(f, carry):
            start = pl.multiple_of(f * cap, cap)
            length = lengths_ref[0, f]

            def tile_of(slot, c):
                row, at = 8 * (c // (tiles // 2)), (c % (tiles // 2)) * LANES
                return blocks[e, slot, :, at : at + LANES].astype(jnp.float32)[row : row + 8]

            for b, spot, other in partner_tiles(lambda c: tile_of(4 + f, c), start):
                live = lane + b * LANES < length
                image[:, spot] = jnp.where(live, tile_of(f, b) + other, 0.0)
            return carry

        lax.fori_loop(0, 4, assemble, 0)

    gather_finish(0)
    await_bytes(coarse.at[pl.ds(0, 4)], coarse_recv)
    coeffs = coefficients(0)
    for f in range(4):
        out_ref[:, face(f)] = correction(coeffs, f)
    op_copy.wait()
    exchange(0, product(out_ref[...]))
    image[...] = known[...] - image[...]

    gather_start(1, row_of(dots(image[...])))
    gather_finish(1)
    coeffs = coefficients(1)
    for f in range(4):
        resid[:, face(f)] = image[:, face(f)] - correction(coeffs, f)

    scaled = weight[...] * resid[...]
    gather_start(2, row_of(dots(scaled) + [dot(resid[...], scaled)]))
    gather_finish(2)
    coeffs = coefficients(2)
    resid_dot = dot_total(2)
    for f in range(4):
        direct[:, face(f)] = weight[:, face(f)] * resid[:, face(f)] - correction(coeffs, f)
    exchange(1, product(direct[...]))
    gather_start(3, row_of(dots(image[...]) + [dot(direct[...], image[...])]))
    gather_finish(3)
    coeffs = coefficients(3)
    step = resid_dot / dot_total(3)
    for f in range(4):
        out_ref[:, face(f)] = out_ref[:, face(f)] + step * direct[:, face(f)]
        corrected = image[:, face(f)] - correction(coeffs, f)
        resid[:, face(f)] = resid[:, face(f)] - step * corrected

    scaled = weight[...] * resid[...]
    gather_start(4, row_of(dots(scaled) + [dot(resid[...], scaled)]))
    gather_finish(4)
    coeffs = coefficients(4)
    previous, resid_dot = resid_dot, dot_total(4)
    ratio = resid_dot / previous
    for f in range(4):
        projected = weight[:, face(f)] * resid[:, face(f)] - correction(coeffs, f)
        direct[:, face(f)] = projected + ratio * direct[:, face(f)]
    rows = product(direct[...]).astype(jnp.bfloat16).astype(jnp.float32)
    mine = direct[:, pl.ds(pl.multiple_of(gz * cap, cap), cap)]
    peers[pl.ds(gz, 1), :] = row_of([(modes, 2.0 * jnp.sum(mine * rows, axis=1, keepdims=True))])
    spot = peers.at[pl.ds(gz, 1)]
    for target in peer_list:
        send(spot, spot, peer_send, peer_recv, target)
    await_bytes(peers.at[pl.ds(0, nz - 1)], peer_recv)
    gather_start(5, jnp.sum(peers[...], axis=0, keepdims=True))
    gather_finish(5)
    step = resid_dot / dot_total(5)
    for f in range(4):
        out_ref[:, face(f)] = out_ref[:, face(f)] + step * direct[:, face(f)]

    await_bytes(faces_out, setup_send)
    await_bytes(coarse.at[pl.ds(0, 4)], coarse_send)
    await_bytes(peers.at[pl.ds(0, nz - 1)], peer_send)
    for g in range(GATHERS):
        await_bytes(plane.at[g, pl.ds(0, plane_size - 1)], plane_send.at[g])
        await_bytes(column.at[g, :, pl.ds(0, (chips - 1) * LANES)], column_send.at[g])
    for e in range(PRODUCTS):
        await_bytes(blocks.at[e, pl.ds(0, 7)], block_send.at[e])


def solution(mesh):
    sizes = tuple(mesh.shape[axis] for axis in ("gx", "gy", "gz"))
    chips, plane_size = sizes[0] // 2, 2 * sizes[1]

    def shards(
        operator,
        rhs_parts,
        stiffness,
        traces,
        coarse_inverse,
        rigid_loads,
        face_lengths,
        face_order,
        mode_count,
    ):
        rows, order = operator.shape[2:]
        load_count = rhs_parts.shape[2]
        modes = traces.shape[2]
        cap = face_order.shape[3]
        padded = chips * LANES
        f32, i32 = jnp.float32, jnp.int32
        vmem = pl.BlockSpec(memory_space=pltpu.VMEM)
        smem = pl.BlockSpec(memory_space=pltpu.SMEM)
        vector = pltpu.VMEM((load_count, order), f32)
        dma = pltpu.SemaphoreType.DMA
        result = pl.pallas_call(
            functools.partial(kernel, sizes),
            out_shape=jax.ShapeDtypeStruct((load_count, order), f32),
            in_specs=[pl.BlockSpec(memory_space=pl.ANY)] + [vmem] * 5 + [smem, vmem, smem],
            out_specs=vmem,
            scratch_shapes=[
                pltpu.VMEM((rows, order), jnp.bfloat16),
                pltpu.VMEM((4, 16, cap), f32),
                pltpu.VMEM((4, 16, cap), f32),
                pltpu.VMEM((8, coarse_inverse.shape[3]), f32),
                pltpu.VMEM((5, 8, padded), f32),
                pltpu.VMEM((GATHERS, plane_size, LANES), f32),
                pltpu.VMEM((GATHERS, 8, padded), f32),
                pltpu.VMEM((sizes[2], LANES), f32),
                pltpu.VMEM((PRODUCTS, 8, 16, cap // 2), jnp.bfloat16),
                pltpu.VMEM((8, order), i32),
                pltpu.VMEM((8, order), i32),
            ]
            + [vector] * 7
            + [
                dma,
                dma,
                dma,
                dma,
                dma,
                dma((GATHERS,)),
                dma((GATHERS,)),
                dma((GATHERS,)),
                dma((GATHERS,)),
                dma,
                dma,
                dma((PRODUCTS,)),
                dma((PRODUCTS,)),
            ],
            compiler_params=pltpu.CompilerParams(
                collective_id=0, has_side_effects=True, vmem_limit_bytes=40 << 20
            ),
        )(
            operator[0, 0],
            rhs_parts[0, 0],
            stiffness[0],
            traces[0, 0],
            coarse_inverse[0, 0],
            rigid_loads[0, 0],
            face_lengths[0],
            face_order[0, 0],
            mode_count,
        )
        return result[None, None]

    in_specs = (
        P("gx", "gy", "gz", None),
        P("gx", "gy", None, None),
        P("gx", "gy", None),
        P("gx", "gy", None, None),
        P("gx", "gy", None, None),
        P("gx", "gy", None, None),
        P("gx", "gy", None),
        P("gx", "gy", None, None),
        P("gx", "gy"),
    )
    out_specs = P("gx", "gy", None, None)
    return jax.shard_map(shards, mesh=mesh, in_specs=in_specs, out_specs=out_specs, check_vma=False)
```

time: 2320 us -> 114 us (0.05)
  blocking collectives: 2090 us -> 0 us
  starting transfers between devices: 108 us -> 0 us
  Pallas kernels: 0 us -> 104 us
  local copies, waits for them, and re-layouts: 82.2 us -> 8.27 us
    unnamed x3 -> x0, blocking collectives: 1460 us -> none
    all_gather x8 -> x0, blocking collectives: 622 us -> none  [the longest x5 594 us: coarse_step(): lax.all_gather(local_coarse[None], ('gx', 'gy'), axis=0, tiled=True)]
    ppermute x32 -> x0, starting transfers between devices: 108 us -> none  [the longest x16 56.9 us: with_halo(): lax.ppermute(lax.slice_in_dim(block, block.shape[dim] - width, None, axis...]
    pallas_call x0 -> x1, Pallas kernels: none -> 104 us  [shards(): pl.pallas_call(functools.partial(kernel, sizes), out_shape=jax.ShapeDtype...]
    gather x16 -> x0, local copies, waits for them, and re-layouts: 72.8 us -> none  [partner(): return jnp.take(facing, flat_slots, axis=1)]
  transfers between devices with their start and end apart: 32 -> 0, of which waited for: 3 -> 0; matrix products, arithmetic and copies ran while one was open for 0% -> 0% of each run, Pallas kernels for 0% -> 0%
where the time goes in v1:
time: 114 us; the launch traced here: 113 us
  Pallas kernels  104 us (91%)
  local copies, waits for them, and re-layouts  8.27 us (7%)
    pallas_call x1, Pallas kernels, shards(): pl.pallas_call(functools.partial(kernel, sizes), out_shape=jax.ShapeDtype...  104 us
    unnamed x14, local copies, waits for them, and re-layouts  8.27 us

profile of v1, /device:TPU:1, one launch (start us, length us, event | category | flops | bytes accessed | tf_op | source)
XLA Modules:
  0.0 113.2 jit_solution(10336908506366329135)
XLA Ops:
  0.7 0.7 copy.18
  1.3 0.7 copy.17
  2.1 0.9 copy.16
  3.0 0.0 copy-start
  3.0 2.3 %copy-done = bf16[1,1,768,3072]{3,2,1,0:T(8,128)(2,1)S(1)} copy-done((bf16[1,1,768,3072]{3,2,1,0:T(8,128)(2,1)S(1)}, bf16[1,1,768,3072]{3,2,1,0:T(8,128)(2,1)}, u32[]{:S(2)}) %copy-start) | copy-done | bytes 4718616
  5.3 0.0 copy-start.1
  5.3 0.9 copy-done.1
  6.2 0.0 copy-start.2
  6.2 0.7 copy-done.2
  6.9 0.0 copy-start.3
  6.9 0.7 copy-done.3
  7.6 0.0 copy-start.4
  7.6 0.7 copy-done.4
  8.3 104.3 %shard_map.91 = f32[8,3072]{1,0:T(8,128)S(1)} custom-call(bf16[768,3072]{1,0:T(8,128)(2,1)S(1)} %bitcast.15, f32[8,3072]{1,0:T(8,128)S(1)} %bitcast.19, f32[1,3072]{1,0:T(1,128)S(1)} %bitcast.21, f32[6,3072]{1,0:T(8,128)S(1)} %bitcast.17, f32[6,1152]{1,0:T(8,128)S(1)} %bitcast.18, f32[6,8]{1,0:T(8,128)S(1)} %bitcast.20, s32[1,4]{1,0:T(1,128)S(1)} %bitcast.23, ...), custom_call_target="tpu_custom_call" | custom-call | tf_op jit(solution)/shard_map/pallas_call | solution.py:389
  112.6 0.6 copy.21
Async XLA Ops:
  3.0 2.3 %copy-start = (bf16[1,1,768,3072]{3,2,1,0:T(8,128)(2,1)S(1)}, bf16[1,1,768,3072]{3,2,1,0:T(8,128)(2,1)}, u32[]{:S(2)}) copy-start(bf16[1,1,768,3072]{3,2,1,0:T(8,128)(2,1)} %param.9) | copy-start | bytes 14155780
  5.3 0.9 copy-start.1
  6.2 0.7 copy-start.2
  6.9 0.7 copy-start.3
  7.6 0.7 copy-start.4

commit v2 on v1

v2 whole, which is shorter than its diff:
```python
import functools

import jax
import jax.numpy as jnp
from jax import lax
from jax.experimental import pallas as pl
from jax.experimental.pallas import tpu as pltpu
from jax.sharding import PartitionSpec as P

MESH = pl.DeviceIdType.MESH
GATHERS = 5
PRODUCTS = 2
LANES = 128
STEPS = ((0, 0), (-1, 0), (1, 0), (0, -1), (0, 1))
OFFSETS = STEPS + ((-2, 0), (2, 0), (0, -2), (0, 2), (-1, -1), (-1, 1), (1, -1), (1, 1))


def kernel(
    sizes,
    op_ref,
    rhs_ref,
    stiff_ref,
    traces_ref,
    inverse_ref,
    loads_ref,
    lengths_ref,
    order_ref,
    count_ref,
    out_ref,
    op_v,
    faces_out,
    faces_in,
    rows_pad,
    loads_in,
    loads_pad,
    lengths,
    order_v,
    counts,
    coarse,
    plane,
    column,
    everyone,
    gathered,
    peers,
    pieces,
    tiles_t,
    mixing,
    blocks,
    op_modes,
    lo_ref,
    hi_ref,
    own_e,
    near_e,
    weight,
    known,
    image,
    resid,
    scaled,
    direct,
    second,
    change,
    product_a,
    product_b,
    product_c,
    op_sem,
    in_sem,
    faces_send,
    faces_recv,
    coarse_send,
    coarse_recv,
    plane_send,
    plane_recv,
    column_send,
    column_recv,
    all_send,
    all_recv,
    peer_send,
    peer_recv,
    piece_send,
    piece_recv,
    tile_send,
    tile_recv,
    block_send,
    block_recv,
):
    nx, ny, nz = sizes
    cap = order_ref.shape[1]
    order = rhs_ref.shape[1]
    tiles = cap // LANES
    modes = traces_ref.shape[0]
    chips = nx // 2
    plane_size = 2 * ny
    spread = plane_size * modes
    gx, gy, gz = lax.axis_index("gx"), lax.axis_index("gy"), lax.axis_index("gz")
    chip, core = gx // 2, gx % 2
    f32 = jnp.float32

    def near(face, z):
        sign = 2 * (face % 2) - 1
        along_x = 1 - face // 2
        return (
            lax.rem(gx + along_x * sign + nx, nx),
            lax.rem(gy + (1 - along_x) * sign + ny, ny),
            z,
        )

    def opposite(face):
        return face + 1 - 2 * (face % 2)

    def shifted(dx, dy):
        return (lax.rem(gx + dx + nx, nx), lax.rem(gy + dy + ny, ny), gz)

    def outward(count):
        return [count // 2 + ((j + 1) // 2) * (1 - 2 * (j % 2)) for j in range(count)]

    peer_list = [(gx, gy, lax.rem(gz + k, nz)) for k in (2, 1, 3)]
    plane_list = [
        (chip * 2 + lax.rem(core + 1 - c, 2), lax.rem(gy + k, ny), gz)
        for k in outward(ny)
        for c in range(2)
        if (c == 0) or k
    ]
    column_list = [(lax.rem(gx + 2 * k, nx), gy, gz) for k in outward(chips) if k]
    product_list = [near(gz, k) for k in range(nz)]
    source_list = [near(f, opposite(f)) for f in range(4)]

    op_copy = pltpu.make_async_copy(op_ref, op_v, op_sem)

    def face(f):
        return slice(f * cap, (f + 1) * cap)

    def fetch(src, dst, sem):
        pltpu.make_async_copy(src, dst, sem).start()

    barrier = pltpu.get_barrier_semaphore()
    greeted = (
        [shifted(dx, dy) for dx, dy in OFFSETS[1:]] + peer_list + plane_list + column_list + source_list
    )
    for target in greeted:
        pl.semaphore_signal(barrier, inc=1, device_id=target, device_id_type=MESH)

    fetch(loads_ref, loads_in, in_sem.at[0])
    fetch(count_ref, counts, in_sem.at[1])
    fetch(lengths_ref, lengths, in_sem.at[2])
    fetch(order_ref, order_v, in_sem.at[3])
    for f in range(4):
        spot = pl.ds(f * cap, cap)
        for m in range(modes):
            fetch(traces_ref.at[m, :, spot], faces_out.at[f, pl.ds(m, 1)], in_sem.at[4])
        fetch(stiff_ref.at[:, spot], faces_out.at[f, pl.ds(modes, 1)], in_sem.at[4])
        fetch(rhs_ref.at[:, spot], faces_out.at[f, pl.ds(8, 8)], in_sem.at[5])
    for m in range(modes):
        fetch(inverse_ref.at[m], rows_pad.at[pl.ds(m, 1)], in_sem.at[6])
    op_copy.start()

    sub = lax.broadcasted_iota(jnp.int32, (8, LANES), 0)
    lane = lax.broadcasted_iota(jnp.int32, (8, LANES), 1)

    def send(src, dst, send_sem, recv_sem, target):
        pltpu.make_async_remote_copy(
            src_ref=src,
            dst_ref=dst,
            send_sem=send_sem,
            recv_sem=recv_sem,
            device_id=target,
            device_id_type=MESH,
        ).start()

    def await_bytes(ref, sem):
        pltpu.make_async_copy(ref, ref, sem).wait()

    def share(ref, send_sem, recv_sem):
        mine, facing = ref.at[pl.ds(gz, 1)], ref.at[pl.ds(4 + opposite(gz), 1)]
        for target in product_list:
            send(mine, facing, send_sem, recv_sem, target)
        for target in peer_list:
            send(mine, mine, send_sem, recv_sem, target)

    def take(values, index):
        return jnp.take_along_axis(values, index, axis=1, mode="promise_in_bounds")

    def fold(x):
        total = x[:, :LANES]
        for c in range(1, x.shape[1] // LANES):
            total = total + x[:, c * LANES : (c + 1) * LANES]
        return total

    def across(x):
        return jnp.sum(x, axis=1, keepdims=True)

    def row_of(columns):
        total = jnp.zeros((8, LANES), f32)
        for j, value in enumerate(columns):
            total = total + jnp.where(lane == 8 * j + sub, value, 0.0)
        return jnp.sum(total, axis=0, keepdims=True)

    pick = jnp.minimum(8 * (lane % modes) + sub, LANES - 1)
    my_slot = core * ny + gy
    my_place = gx * ny + gy

    def tile_of_rows(rows):
        tile = take(jnp.broadcast_to(rows(0), (8, LANES)), pick)
        for s in range(1, plane_size):
            found = take(jnp.broadcast_to(rows(s), (8, LANES)), pick)
            tile = jnp.where(lane >= s * modes, found, tile)
        return tile

    def near_gather(row):
        plane[pl.ds(my_slot, 1), :] = row
        mine = plane.at[pl.ds(my_slot, 1)]
        for target in plane_list:
            send(mine, mine, plane_send, plane_recv, target)

    def near_gather_on():
        await_bytes(plane.at[pl.ds(0, plane_size - 1)], plane_recv)
        spot = pl.ds(pl.multiple_of(chip * LANES, LANES), LANES)
        column[:, spot] = tile_of_rows(lambda s: plane[s : s + 1, :])
        mine = column.at[:, spot]
        for target in column_list:
            send(mine, mine, column_send, column_recv, target)

    def near_gather_end():
        await_bytes(column.at[:, pl.ds(0, (chips - 1) * LANES)], column_recv)
        return column[...]

    def gather_start(g, row):
        everyone[g, pl.ds(my_place, 1), :] = row
        mine = everyone.at[g, pl.ds(my_place, 1)]

        def one_plane(i, carry):
            away = chips // 2 + ((i + 1) // 2) * (1 - 2 * (i % 2))
            there = lax.rem(chip + away, chips)
            for k in outward(ny):
                for c in (1, 0):
                    target = (there * 2 + lax.rem(core + c, 2), lax.rem(gy + k, ny), gz)
                    send(mine, mine, all_send.at[g], all_recv.at[g], target)
            return carry

        lax.fori_loop(0, chips - 1, one_plane, 0)
        for target in plane_list:
            send(mine, mine, all_send.at[g], all_recv.at[g], target)

    def gather_wait(g):
        await_bytes(everyone.at[g, pl.ds(0, nx * ny - 1)], all_recv.at[g])

    def gather_end(g):
        gather_wait(g)
        for z in range(chips):
            at = z * plane_size
            gathered[:, z * LANES : (z + 1) * LANES] = tile_of_rows(
                lambda s: everyone[g, at + s : at + s + 1, :]
            )
        return gathered[...]

    def dot_totals(g, wanted):
        total = everyone[g, 0:8, :]
        for c in range(1, nx * ny // 8):
            total = total + everyone[g, 8 * c : 8 * (c + 1), :]
        total = jnp.broadcast_to(jnp.sum(total, axis=0, keepdims=True), (8, LANES))
        return [across(jnp.where(lane == 8 * j + sub, total, 0.0)) for j in wanted]

    def coefficients(values, count):
        return [
            [across(fold(values * coarse[u, m : m + 1, :])) for m in range(modes)]
            for u in range(count)
        ]

    def correction(coeffs, f):
        total = coeffs[0][0] * own_e[0:1, face(f)]
        total = total + coeffs[1 + f][0] * near_e[0:1, face(f)]
        for m in range(1, modes):
            total = total + coeffs[0][m] * own_e[m : m + 1, face(f)]
            total = total + coeffs[1 + f][m] * near_e[m : m + 1, face(f)]
        return total

    def corrected_product(coeffs):
        total = coeffs[0][0] * op_modes[0:1, :]
        for u in range(5):
            for m in range(modes):
                if u or m:
                    total = total + coeffs[u][m] * op_modes[8 * u + m : 8 * u + m + 1, :]
        return total

    where_of = {offset: u for u, offset in enumerate(OFFSETS)}
    own_lane = (lane % 8 == sub) & (lane < 8 * modes)

    def mixed_row(coeffs):
        total = jnp.zeros((8, LANES), f32)
        for t, at in enumerate(STEPS):
            for u, step in enumerate(STEPS):
                found = coeffs[where_of[(at[0] + step[0], at[1] + step[1])]]
                for m in range(modes):
                    total = total + found[m] * mixing[t, 8 * u + m : 8 * u + m + 1, :]
        return jnp.sum(jnp.where(own_lane, total, 0.0), axis=0, keepdims=True)

    def partner_tiles(load, start):
        given = [load(c) for c in range(tiles)]
        for b in range(tiles):
            spot = pl.ds(pl.multiple_of(start + b * LANES, LANES), LANES)
            low, high = lo_ref[:, spot], hi_ref[:, spot]
            result = take(given[0], low)
            for c in range(1, tiles):
                result = jnp.where(high == c, take(given[c], low), result)
            yield b, spot, result

    def split(x):
        high = x.astype(jnp.bfloat16)
        low = (x - high.astype(f32)).astype(jnp.bfloat16)
        return jnp.concatenate([high.astype(f32), low.astype(f32)], axis=0).astype(jnp.bfloat16)

    def times(left, columns):
        return lax.dot_general(
            left, op_v[:, columns], (((1,), (1,)), ((), ())), preferred_element_type=f32
        )

    def product(vector):
        total = jnp.zeros((8, cap), f32)
        for f in range(4):
            both = times(split(vector[:, face(f)]), face(f))
            total = total + both[:8] + both[8:]
        return total

    def exchange_start(e, rows):
        blocks[e, pl.ds(gz, 1)] = rows.reshape(1, 8, cap)
        share(blocks.at[e], block_send.at[e], block_recv.at[e])

    def exchange_end(e, use):
        await_bytes(blocks.at[e, pl.ds(0, 7)], block_recv.at[e])

        def assemble(f, carry):
            start = pl.multiple_of(f * cap, cap)
            length = lengths[0, f]

            def tile_of(slot, c):
                return blocks[e, slot, :, c * LANES : (c + 1) * LANES]

            for b, spot, other in partner_tiles(lambda c: tile_of(4 + f, c), start):
                live = lane + b * LANES < length
                use(spot, jnp.where(live, tile_of(f, b) + other, 0.0))
            return carry

        lax.fori_loop(0, 4, assemble, 0)

    await_bytes(loads_in, in_sem.at[0])
    await_bytes(counts, in_sem.at[1])
    count = counts[0, 0]
    loads_pad[...] = jnp.zeros_like(loads_pad)
    for m in range(modes):
        loads_pad[m : m + 1, 0 : loads_ref.shape[2]] = loads_in[m]
    loads_tile = jnp.where(sub < count, loads_pad[...], 0.0)
    first = jnp.zeros((8, LANES), f32)
    for m in range(modes):
        only = jnp.where(sub == m, loads_tile, 0.0)
        first = first + (only if m == 0 else pltpu.roll(only, 8 * m, axis=1))
    first = jnp.sum(first, axis=0, keepdims=True)

    await_bytes(faces_out.at[:, pl.ds(0, modes + 1)], in_sem.at[4])
    await_bytes(faces_out.at[:, pl.ds(8, 8)], in_sem.at[5])
    live_mode = lax.broadcasted_iota(jnp.int32, (modes, cap), 0) < count
    for f in range(4):
        faces_out[f, 0:modes, :] = jnp.where(live_mode, faces_out[f, 0:modes, :], 0.0)
        faces_out[f, modes + 1 : 8, :] = jnp.zeros((7 - modes, cap), f32)

    pl.semaphore_wait(barrier, len(greeted))

    near_gather(first)
    for f in range(4):
        send(
            faces_out.at[f], faces_in.at[f + 1 - 2 * (f % 2)], faces_send, faces_recv, near(f, gz)
        )

    await_bytes(rows_pad.at[pl.ds(0, modes)], in_sem.at[6])
    rows_pad[modes:8, :] = jnp.zeros((8 - modes, rows_pad.shape[1]), f32)
    for z in range(chips):
        start = z * spread
        base, shift = start // LANES, start % LANES
        chunk = rows_pad[:, base * LANES : (base + 1) * LANES]
        if shift:
            chunk = pltpu.roll(chunk, LANES - shift, axis=1)
            if LANES - shift < spread:
                after = rows_pad[:, (base + 1) * LANES : (base + 2) * LANES]
                after = pltpu.roll(after, LANES - shift, axis=1)
                chunk = jnp.where(lane < LANES - shift, chunk, after)
        coarse[0, :, z * LANES : (z + 1) * LANES] = jnp.where(lane < spread, chunk, 0.0)
    for u in range(1, len(OFFSETS)):
        dx, dy = OFFSETS[u]
        send(
            coarse.at[0, pl.ds(0, modes)],
            coarse.at[u, pl.ds(0, modes)],
            coarse_send,
            coarse_recv,
            shifted(-dx, -dy),
        )

    await_bytes(lengths, in_sem.at[2])
    await_bytes(order_v, in_sem.at[3])
    for f in range(4):
        index = jnp.broadcast_to(order_v[f : f + 1, :], (8, cap))
        lo_ref[:, face(f)] = index & (LANES - 1)
        hi_ref[:, face(f)] = index >> 7

    await_bytes(faces_in, faces_recv)

    def setup_face(f, carry):
        start = pl.multiple_of(f * cap, cap)
        length = lengths[0, f]
        for b, spot, other in partner_tiles(
            lambda c: faces_in[f, 0:8, c * LANES : (c + 1) * LANES], start
        ):
            part = slice(b * LANES, (b + 1) * LANES)
            live = lane + b * LANES < length
            mine = faces_out[f, 0:8, part]
            own_e[:, spot] = jnp.where(live & (sub < modes), mine, 0.0)
            near_e[:, spot] = jnp.where(live & (sub < modes), other, 0.0)
            stiff = jnp.broadcast_to((mine + other)[modes : modes + 1, :], (8, LANES))
            weight[:, spot] = jnp.where(live, 1.0 / jnp.where(live, stiff, 1.0), 0.0)
        for b, spot, other in partner_tiles(
            lambda c: faces_in[f, 8:16, c * LANES : (c + 1) * LANES], start
        ):
            part = slice(b * LANES, (b + 1) * LANES)
            live = lane + b * LANES < length
            known[:, spot] = jnp.where(live, faces_out[f, 8:16, part] + other, 0.0)
        return carry

    lax.fori_loop(0, 4, setup_face, 0)
    near_gather_on()

    op_copy.wait()
    own_rows = jnp.zeros((8, cap), f32)
    for f in range(4):
        both = jnp.concatenate([own_e[:, face(f)], near_e[:, face(f)]], axis=0)
        both = times(split(both), face(f))
        both = both[:16] + both[16:]
        own_rows = own_rows + both[:8]
        op_modes[8 * (1 + f) : 8 * (2 + f), :] = both[8:]
    op_modes[0:8, :] = own_rows

    block = pl.ds(pl.multiple_of(gz * cap, cap), cap)
    block_e = jnp.concatenate([own_e[:, block], near_e[:, block]], axis=0)
    part = lax.dot_general(
        op_modes[...],
        block_e,
        (((1,), (1,)), ((), ())),
        precision=lax.Precision.HIGHEST,
        preferred_element_type=f32,
    )
    wide = jnp.concatenate([part, jnp.zeros((40, LANES - 16), f32)], axis=1)
    tiles_t[pl.ds(gz, 1)] = wide.reshape(1, 40, LANES)
    share(tiles_t, tile_send, tile_recv)
    known_dots = [
        across(sum(fold(known[:, face(f)] * own_e[m : m + 1, face(f)]) for f in range(4)))
        for m in range(modes)
    ]
    known_row = row_of(known_dots)
    await_bytes(tiles_t.at[pl.ds(0, 7)], tile_recv)
    spread_own = jnp.minimum(lane // 8, 7)
    for u in range(5):
        rows = slice(8 * u, 8 * (u + 1))
        own_sum = tiles_t[0, rows, :] + tiles_t[1, rows, :] + tiles_t[2, rows, :] + tiles_t[3, rows, :]
        mixing[0, rows, :] = take(own_sum, spread_own)
        for f in range(4):
            mixing[1 + f, rows, :] = take(tiles_t[4 + f, rows, :], spread_own + 8)

    await_bytes(coarse.at[pl.ds(0, len(OFFSETS) - 1), pl.ds(0, modes)], coarse_recv)
    coeffs = coefficients(near_gather_end(), len(OFFSETS))
    gather_start(0, known_row - mixed_row(coeffs))
    exchange_start(0, corrected_product(coeffs))
    for f in range(4):
        out_ref[:, face(f)] = correction(coeffs, f)

    def gap(spot, tile):
        image[:, spot] = known[:, spot] - tile

    exchange_end(0, gap)

    coeffs = coefficients(gather_end(0), 5)
    sums = [jnp.zeros((8, LANES), f32) for _ in range(modes + 1)]
    for f in range(4):
        left = image[:, face(f)] - correction(coeffs, f)
        right = weight[:, face(f)] * left
        resid[:, face(f)] = left
        scaled[:, face(f)] = right
        for m in range(modes):
            sums[m] = sums[m] + fold(right * own_e[m : m + 1, face(f)])
        sums[modes] = sums[modes] + fold(left * right)
    gather_start(1, row_of([across(x) for x in sums]))

    rows = product(scaled)
    product_a[...] = rows
    parts = [
        across(fold(rows * e[m : m + 1, block])) for e in (own_e, near_e) for m in range(modes)
    ]
    pieces[pl.ds(gz, 1), :] = row_of(parts)
    share(pieces, piece_send, piece_recv)
    await_bytes(pieces.at[pl.ds(0, 7)], piece_recv)
    found = pieces[...]
    found = jnp.where(sub < 4, found, pltpu.roll(found, LANES - 8 * modes, axis=1))
    found = jnp.where(lane < 8 * modes, found, 0.0)
    found = jnp.sum(found, axis=0, keepdims=True)

    first_coeffs = coefficients(gather_end(1), len(OFFSETS))
    gather_start(2, found - mixed_row(first_coeffs))
    (resid_dot,) = dot_totals(1, (modes,))
    rows = product_a[...] - corrected_product(first_coeffs)
    product_b[...] = rows
    exchange_start(1, rows)
    for f in range(4):
        direct[:, face(f)] = scaled[:, face(f)] - correction(first_coeffs, f)

    def keep(spot, tile):
        image[:, spot] = tile

    exchange_end(1, keep)

    coeffs = coefficients(gather_end(2), 5)
    sums = [jnp.zeros((8, LANES), f32) for _ in range(modes + 3)]
    for f in range(4):
        left = image[:, face(f)] - correction(coeffs, f)
        right = weight[:, face(f)] * left
        change[:, face(f)] = right
        for m in range(modes):
            sums[m] = sums[m] + fold(right * own_e[m : m + 1, face(f)])
        sums[modes] = sums[modes] + fold(direct[:, face(f)] * image[:, face(f)])
        sums[modes + 1] = sums[modes + 1] + fold(resid[:, face(f)] * right)
        sums[modes + 2] = sums[modes + 2] + fold(left * right)
    gather_start(3, row_of([across(x) for x in sums]))
    product_c[...] = product(change)

    change_coeffs = coefficients(gather_end(3), 5)
    curvature, cross, square = dot_totals(3, (modes, modes + 1, modes + 2))
    step = resid_dot / curvature
    next_dot = resid_dot - 2.0 * step * cross + step * step * square
    ratio = next_dot / resid_dot
    coeffs = [
        [a - step * b for a, b in zip(first_coeffs[u], change_coeffs[u], strict=True)]
        for u in range(5)
    ]
    for f in range(4):
        projected = scaled[:, face(f)] - step * change[:, face(f)] - correction(coeffs, f)
        second[:, face(f)] = projected + ratio * direct[:, face(f)]
    rows = product_a[...] - step * product_c[...] - corrected_product(coeffs)
    rows = rows + ratio * product_b[...]
    half = across(fold(second[:, block] * rows))
    peers[pl.ds(gz, 1), :] = row_of([jnp.zeros((8, 1), f32)] * modes + [2.0 * half])
    mine = peers.at[pl.ds(gz, 1)]
    for target in peer_list:
        send(mine, mine, peer_send, peer_recv, target)
    await_bytes(peers.at[pl.ds(0, nz - 1)], peer_recv)
    gather_start(4, jnp.sum(peers[...], axis=0, keepdims=True))
    for f in range(4):
        out_ref[:, face(f)] = out_ref[:, face(f)] + step * direct[:, face(f)]
    gather_wait(4)
    (curvature,) = dot_totals(4, (modes,))
    step = next_dot / curvature
    for f in range(4):
        out_ref[:, face(f)] = out_ref[:, face(f)] + step * second[:, face(f)]

    await_bytes(faces_out, faces_send)
    await_bytes(coarse.at[pl.ds(0, len(OFFSETS) - 1), pl.ds(0, modes)], coarse_send)
    await_bytes(plane.at[pl.ds(0, plane_size - 1)], plane_send)
    await_bytes(column.at[:, pl.ds(0, (chips - 1) * LANES)], column_send)
    await_bytes(peers.at[pl.ds(0, nz - 1)], peer_send)
    await_bytes(pieces.at[pl.ds(0, 7)], piece_send)
    await_bytes(tiles_t.at[pl.ds(0, 7)], tile_send)
    for g in range(GATHERS):
        await_bytes(everyone.at[g, pl.ds(0, nx * ny - 1)], all_send.at[g])
    for e in range(PRODUCTS):
        await_bytes(blocks.at[e, pl.ds(0, 7)], block_send.at[e])


def solution(mesh):
    sizes = tuple(mesh.shape[axis] for axis in ("gx", "gy", "gz"))
    chips, plane_size = sizes[0] // 2, 2 * sizes[1]

    def shards(
        operator,
        rhs_parts,
        stiffness,
        traces,
        coarse_inverse,
        rigid_loads,
        face_lengths,
        face_order,
        mode_count,
    ):
        rows, order = operator.shape[2:]
        load_count = rhs_parts.shape[2]
        modes = traces.shape[2]
        cap = face_order.shape[3]
        padded = chips * LANES
        f32, i32 = jnp.float32, jnp.int32
        anywhere = pl.BlockSpec(memory_space=pl.ANY)
        vector = pltpu.VMEM((load_count, order), f32)
        block = pltpu.VMEM((load_count, cap), f32)
        dma = pltpu.SemaphoreType.DMA

        def by_row(array):
            return jnp.transpose(array[0], (1, 0, 2))

        result = pl.pallas_call(
            functools.partial(kernel, sizes),
            out_shape=jax.ShapeDtypeStruct((load_count, order), f32),
            in_specs=[anywhere] * 9,
            out_specs=pl.BlockSpec(memory_space=pltpu.VMEM),
            scratch_shapes=[
                pltpu.VMEM((rows, order), jnp.bfloat16),
                pltpu.VMEM((4, 16, cap), f32),
                pltpu.VMEM((4, 16, cap), f32),
                pltpu.VMEM((8, coarse_inverse.shape[3]), f32),
                pltpu.VMEM((modes, 1, load_count), f32),
                pltpu.VMEM((8, LANES), f32),
                pltpu.SMEM((1, 4), i32),
                pltpu.VMEM((4, cap), i32),
                pltpu.SMEM((1, 1), i32),
                pltpu.VMEM((len(OFFSETS), 8, padded), f32),
                pltpu.VMEM((plane_size, LANES), f32),
                pltpu.VMEM((8, padded), f32),
                pltpu.VMEM((GATHERS, sizes[0] * sizes[1], LANES), f32),
                pltpu.VMEM((8, padded), f32),
                pltpu.VMEM((sizes[2], LANES), f32),
                pltpu.VMEM((8, LANES), f32),
                pltpu.VMEM((8, 40, LANES), f32),
                pltpu.VMEM((5, 40, LANES), f32),
                pltpu.VMEM((PRODUCTS, 8, 8, cap), f32),
                pltpu.VMEM((40, cap), f32),
                pltpu.VMEM((8, order), i32),
                pltpu.VMEM((8, order), i32),
            ]
            + [vector] * 10
            + [block] * 3
            + [dma, dma((7,))]
            + [dma] * 8
            + [dma((GATHERS,))] * 2
            + [dma] * 6
            + [dma((PRODUCTS,))] * 2,
            compiler_params=pltpu.CompilerParams(
                collective_id=0, has_side_effects=True, vmem_limit_bytes=60 << 20
            ),
        )(
            operator[0, 0],
            rhs_parts[0, 0],
            stiffness[0],
            by_row(traces),
            by_row(coarse_inverse),
            by_row(rigid_loads),
            face_lengths[0],
            face_order[0, 0],
            mode_count,
        )
        return result[None, None]

    in_specs = (
        P("gx", "gy", "gz", None),
        P("gx", "gy", None, None),
        P("gx", "gy", None),
        P("gx", "gy", None, None),
        P("gx", "gy", None, None),
        P("gx", "gy", None, None),
        P("gx", "gy", None),
        P("gx", "gy", None, None),
        P("gx", "gy"),
    )
    out_specs = P("gx", "gy", None, None)
    return jax.shard_map(shards, mesh=mesh, in_specs=in_specs, out_specs=out_specs, check_vma=False)
```

time: 114 us -> 84.8 us (0.74)
  Pallas kernels: 104 us -> 82.4 us
  local copies, waits for them, and re-layouts: 8.27 us -> 1.54 us
    pallas_call x1, Pallas kernels: 104 us -> 82.4 us  [shards(): pl.pallas_call(functools.partial(kernel, sizes), out_shape=jax.ShapeDtype...]
    unnamed x14 -> x1, local copies, waits for them, and re-layouts: 8.27 us -> 1.54 us
where the time goes in v2:
time: 84.8 us; the launch traced here: 84.6 us
  Pallas kernels  82.4 us (97%)
  local copies, waits for them, and re-layouts  1.54 us (2%)
    pallas_call x1, Pallas kernels, shards(): pl.pallas_call(functools.partial(kernel, sizes), out_shape=jax.ShapeDtype...  82.4 us

profile of v2, /device:TPU:1, one launch (start us, length us, event | category | flops | bytes accessed | tf_op | source)
XLA Modules:
  0.0 84.6 jit_solution(8705145323586839566)
XLA Ops:
  0.7 82.4 %shard_map.91 = f32[8,3072]{1,0:T(8,128)} custom-call(bf16[768,3072]{1,0:T(8,128)(2,1)} %bitcast.9, f32[8,3072]{1,0:T(8,128)} %bitcast.11, f32[1,3072]{1,0:T(1,128)} %bitcast.14, f32[6,1,3072]{2,1,0:T(1,128)} %bitcast.12, f32[6,1,1152]{2,1,0:T(1,128)} %bitcast.13, f32[6,1,8]{2,1,0:T(1,128)} %bitcast.16, s32[1,4]{1,0:T(1,128)} %bitcast.17, ...), custom_call_target="tpu_custom_call" | custom-call | tf_op jit(solution)/shard_map/pallas_call | solution.py:600
  83.1 1.5 %copy.12 = f32[1,1,8,3072]{3,2,1,0:T(8,128)} copy(f32[1,1,8,3072]{3,2,1,0:T(8,128)} %bitcast.10) | data formatting | bytes 196608

commit v3 on v2

--- a/solution.py
+++ b/solution.py
@@ -8,7 +8,7 @@
 from jax.sharding import PartitionSpec as P
 
 MESH = pl.DeviceIdType.MESH
-GATHERS = 5
+GATHERS = 4
 PRODUCTS = 2
 LANES = 128
 STEPS = ((0, 0), (-1, 0), (1, 0), (0, -1), (0, 1))
@@ -40,13 +40,17 @@
     plane,
     column,
     everyone,
-    gathered,
     peers,
-    pieces,
     tiles_t,
     mixing,
     blocks,
     op_modes,
+    op_heavy,
+    chunks,
+    plane_sc,
+    parts_out,
+    parts_in,
+    twice,
     lo_ref,
     hi_ref,
     own_e,
@@ -76,12 +80,18 @@
     all_recv,
     peer_send,
     peer_recv,
-    piece_send,
-    piece_recv,
     tile_send,
     tile_recv,
     block_send,
     block_recv,
+    chunk_send,
+    chunk_recv,
+    sc_send,
+    sc_recv,
+    parts_send,
+    parts_recv,
+    twice_send,
+    twice_recv,
 ):
     nx, ny, nz = sizes
     cap = order_ref.shape[1]
@@ -191,17 +201,19 @@
     def row_of(columns):
         total = jnp.zeros((8, LANES), f32)
         for j, value in enumerate(columns):
+            if value is None:
+                continue
             total = total + jnp.where(lane == 8 * j + sub, value, 0.0)
         return jnp.sum(total, axis=0, keepdims=True)
 
     pick = jnp.minimum(8 * (lane % modes) + sub, LANES - 1)
     my_slot = core * ny + gy
-    my_place = gx * ny + gy
-
-    def tile_of_rows(rows):
-        tile = take(jnp.broadcast_to(rows(0), (8, LANES)), pick)
+
+    def tile_of_rows(rows, first=0):
+        at = jnp.minimum(pick + 8 * first, LANES - 1)
+        tile = take(jnp.broadcast_to(rows(0), (8, LANES)), at)
         for s in range(1, plane_size):
-            found = take(jnp.broadcast_to(rows(s), (8, LANES)), pick)
+            found = take(jnp.broadcast_to(rows(s), (8, LANES)), at)
             tile = jnp.where(lane >= s * modes, found, tile)
         return tile
 
@@ -223,9 +235,11 @@
         await_bytes(column.at[:, pl.ds(0, (chips - 1) * LANES)], column_recv)
         return column[...]
 
+    pair = 2 * (chip * ny + gy)
+
     def gather_start(g, row):
-        everyone[g, pl.ds(my_place, 1), :] = row
-        mine = everyone.at[g, pl.ds(my_place, 1)]
+        everyone[g, pl.ds(pair + core, 1), :] = row
+        mine = everyone.at[g, pl.ds(pair + core, 1)]
 
         def one_plane(i, carry):
             away = chips // 2 + ((i + 1) // 2) * (1 - 2 * (i % 2))
@@ -243,14 +257,16 @@
     def gather_wait(g):
         await_bytes(everyone.at[g, pl.ds(0, nx * ny - 1)], all_recv.at[g])
 
-    def gather_end(g):
-        gather_wait(g)
+    def coarse_values(g, first=0):
+        planes = []
         for z in range(chips):
             at = z * plane_size
-            gathered[:, z * LANES : (z + 1) * LANES] = tile_of_rows(
-                lambda s: everyone[g, at + s : at + s + 1, :]
+            planes.append(
+                tile_of_rows(
+                    lambda s: everyone[g, pl.ds(at + 2 * (s % ny) + s // ny, 1), :], first
+                )
             )
-        return gathered[...]
+        return jnp.concatenate(planes, axis=1)
 
     def dot_totals(g, wanted):
         total = everyone[g, 0:8, :]
@@ -273,12 +289,12 @@
             total = total + coeffs[1 + f][m] * near_e[m : m + 1, face(f)]
         return total
 
-    def corrected_product(coeffs):
-        total = coeffs[0][0] * op_modes[0:1, :]
+    def modes_times(ref, coeffs):
+        total = coeffs[0][0] * ref[0:1, :]
         for u in range(5):
             for m in range(modes):
                 if u or m:
-                    total = total + coeffs[u][m] * op_modes[8 * u + m : 8 * u + m + 1, :]
+                    total = total + coeffs[u][m] * ref[8 * u + m : 8 * u + m + 1, :]
         return total
 
     where_of = {offset: u for u, offset in enumerate(OFFSETS)}
@@ -321,7 +337,8 @@
         return total
 
     def exchange_start(e, rows):
-        blocks[e, pl.ds(gz, 1)] = rows.reshape(1, 8, cap)
+        packed = jnp.concatenate([rows[:, : cap // 2], rows[:, cap // 2 :]], axis=0)
+        blocks[e, pl.ds(gz, 1)] = packed.astype(jnp.bfloat16).reshape(1, 16, cap // 2)
         share(blocks.at[e], block_send.at[e], block_recv.at[e])
 
     def exchange_end(e, use):
@@ -332,7 +349,9 @@
             length = lengths[0, f]
 
             def tile_of(slot, c):
-                return blocks[e, slot, :, c * LANES : (c + 1) * LANES]
+                row, at = 8 * (c // (tiles // 2)), c % (tiles // 2) * LANES
+                both = blocks[e, slot, :, at : at + LANES].astype(f32)
+                return both[row : row + 8]
 
             for b, spot, other in partner_tiles(lambda c: tile_of(4 + f, c), start):
                 live = lane + b * LANES < length
@@ -392,6 +411,19 @@
             shifted(-dx, -dy),
         )
 
+    chunks[pl.ds(chip, 1)] = coarse[
+        0, :, pl.ds(pl.multiple_of(chip * LANES, LANES), LANES)
+    ].reshape(1, 8, LANES)
+    for k in outward(chips):
+        if k:
+            there = lax.rem(chip + k, chips)
+            send(
+                coarse.at[0, :, pl.ds(pl.multiple_of(there * LANES, LANES), LANES)],
+                chunks.at[chip],
+                chunk_send,
+                chunk_recv,
+                (there * 2 + core, gy, gz),
+            )
     await_bytes(lengths, in_sem.at[2])
     await_bytes(order_v, in_sem.at[3])
     for f in range(4):
@@ -425,15 +457,20 @@
     lax.fori_loop(0, 4, setup_face, 0)
     near_gather_on()
 
+    def modes_product(ref, heavy):
+        own_rows = jnp.zeros((8, cap), f32)
+        for f in range(4):
+            both = [own_e[:, face(f)], near_e[:, face(f)]]
+            if heavy:
+                both = [weight[:, face(f)] * e for e in both]
+            both = times(split(jnp.concatenate(both, axis=0)), face(f))
+            both = both[:16] + both[16:]
+            own_rows = own_rows + both[:8]
+            ref[8 * (1 + f) : 8 * (2 + f), :] = both[8:]
+        ref[0:8, :] = own_rows
+
     op_copy.wait()
-    own_rows = jnp.zeros((8, cap), f32)
-    for f in range(4):
-        both = jnp.concatenate([own_e[:, face(f)], near_e[:, face(f)]], axis=0)
-        both = times(split(both), face(f))
-        both = both[:16] + both[16:]
-        own_rows = own_rows + both[:8]
-        op_modes[8 * (1 + f) : 8 * (2 + f), :] = both[8:]
-    op_modes[0:8, :] = own_rows
+    modes_product(op_modes, False)
 
     block = pl.ds(pl.multiple_of(gz * cap, cap), cap)
     block_e = jnp.concatenate([own_e[:, block], near_e[:, block]], axis=0)
@@ -464,7 +501,7 @@
     await_bytes(coarse.at[pl.ds(0, len(OFFSETS) - 1), pl.ds(0, modes)], coarse_recv)
     coeffs = coefficients(near_gather_end(), len(OFFSETS))
     gather_start(0, known_row - mixed_row(coeffs))
-    exchange_start(0, corrected_product(coeffs))
+    exchange_start(0, modes_times(op_modes, coeffs))
     for f in range(4):
         out_ref[:, face(f)] = correction(coeffs, f)
 
@@ -473,7 +510,25 @@
 
     exchange_end(0, gap)
 
-    coeffs = coefficients(gather_end(0), 5)
+    quarter = chips // nz * LANES
+    share_of = pl.ds(pl.multiple_of(gz * quarter, LANES), quarter)
+    part_sc = jnp.zeros((8, quarter), f32)
+    for m in range(modes):
+        own_sum = jnp.zeros((8, LANES), f32)
+        for f in range(4):
+            heavy = own_e[:, face(f)] * weight[:, face(f)]
+            own_sum = own_sum + fold(heavy * own_e[m : m + 1, face(f)])
+            near_sum = across(fold(heavy * near_e[m : m + 1, face(f)]))
+            part_sc = part_sc + near_sum * coarse[1 + f, m : m + 1, share_of]
+        part_sc = part_sc + across(own_sum) * coarse[0, m : m + 1, share_of]
+    plane_sc[:, modes:8, :] = jnp.zeros((plane_size, 8 - modes, quarter), f32)
+    plane_sc[pl.ds(my_slot, 1), 0:modes] = part_sc[:modes].reshape(1, modes, quarter)
+    mine = plane_sc.at[my_slot, pl.ds(0, modes)]
+    for target in plane_list:
+        send(mine, mine, sc_send, sc_recv, target)
+
+    gather_wait(0)
+    coeffs = coefficients(coarse_values(0), 5)
     sums = [jnp.zeros((8, LANES), f32) for _ in range(modes + 1)]
     for f in range(4):
         left = image[:, face(f)] - correction(coeffs, f)
@@ -485,25 +540,39 @@
         sums[modes] = sums[modes] + fold(left * right)
     gather_start(1, row_of([across(x) for x in sums]))
 
-    rows = product(scaled)
-    product_a[...] = rows
-    parts = [
-        across(fold(rows * e[m : m + 1, block])) for e in (own_e, near_e) for m in range(modes)
-    ]
-    pieces[pl.ds(gz, 1), :] = row_of(parts)
-    share(pieces, piece_send, piece_recv)
-    await_bytes(pieces.at[pl.ds(0, 7)], piece_recv)
-    found = pieces[...]
-    found = jnp.where(sub < 4, found, pltpu.roll(found, LANES - 8 * modes, axis=1))
-    found = jnp.where(lane < 8 * modes, found, 0.0)
-    found = jnp.sum(found, axis=0, keepdims=True)
-
-    first_coeffs = coefficients(gather_end(1), len(OFFSETS))
-    gather_start(2, found - mixed_row(first_coeffs))
+    product_a[...] = product(scaled)
+    modes_product(op_heavy, True)
+
+    await_bytes(chunks.at[pl.ds(0, chips - 1)], chunk_recv)
+    await_bytes(plane_sc.at[pl.ds(0, plane_size - 1), pl.ds(0, modes)], sc_recv)
+    wide_pick = lane // 8 * modes + jnp.minimum(lane % 8, modes - 1)
+    left = [jnp.where(lane % 8 < modes, take(chunks[z], wide_pick), 0.0) for z in range(chips)]
+    terms = lax.dot_general(
+        jnp.concatenate(left, axis=0),
+        plane_sc[...].reshape(plane_size * 8, quarter),
+        (((1,), (0,)), ((), ())),
+        precision=lax.Precision.HIGHEST,
+        preferred_element_type=f32,
+    )
+    parts_out[...] = terms.reshape(chips, 8, quarter)
+    parts_in[pl.ds(chip, 1)] = parts_out[pl.ds(chip, 1)]
+    for k in outward(chips):
+        if k:
+            there = lax.rem(chip + k, chips)
+            send(
+                parts_out.at[there, pl.ds(0, modes)],
+                parts_in.at[chip, pl.ds(0, modes)],
+                parts_send,
+                parts_recv,
+                (there * 2 + core, gy, gz),
+            )
+
+    gather_wait(1)
+    first_coeffs = coefficients(coarse_values(1), 5)
+    rows = product_a[...] - modes_times(op_modes, first_coeffs)
+    exchange_start(1, rows)
+    product_b[...] = rows
     (resid_dot,) = dot_totals(1, (modes,))
-    rows = product_a[...] - corrected_product(first_coeffs)
-    product_b[...] = rows
-    exchange_start(1, rows)
     for f in range(4):
         direct[:, face(f)] = scaled[:, face(f)] - correction(first_coeffs, f)
 
@@ -512,58 +581,102 @@
 
     exchange_end(1, keep)
 
-    coeffs = coefficients(gather_end(2), 5)
-    sums = [jnp.zeros((8, LANES), f32) for _ in range(modes + 3)]
-    for f in range(4):
-        left = image[:, face(f)] - correction(coeffs, f)
+    sums = [jnp.zeros((8, LANES), f32) for _ in range(2 * modes + 2)]
+    for f in range(4):
+        left = image[:, face(f)]
         right = weight[:, face(f)] * left
         change[:, face(f)] = right
         for m in range(modes):
-            sums[m] = sums[m] + fold(right * own_e[m : m + 1, face(f)])
-        sums[modes] = sums[modes] + fold(direct[:, face(f)] * image[:, face(f)])
-        sums[modes + 1] = sums[modes + 1] + fold(resid[:, face(f)] * right)
-        sums[modes + 2] = sums[modes + 2] + fold(left * right)
-    gather_start(3, row_of([across(x) for x in sums]))
+            sums[m] = sums[m] + fold(left * own_e[m : m + 1, face(f)])
+            sums[modes + m] = sums[modes + m] + fold(right * own_e[m : m + 1, face(f)])
+        sums[2 * modes] = sums[2 * modes] + fold(direct[:, face(f)] * left)
+        sums[2 * modes + 1] = sums[2 * modes + 1] + fold(scaled[:, face(f)] * left)
+    sums = [across(x) for x in sums]
+    for m in range(modes):
+        sums[2 * modes + 1] = sums[2 * modes + 1] - 2.0 * sums[m] * first_coeffs[0][m]
+    gather_start(2, row_of(sums))
     product_c[...] = product(change)
 
-    change_coeffs = coefficients(gather_end(3), 5)
-    curvature, cross, square = dot_totals(3, (modes, modes + 1, modes + 2))
+    await_bytes(parts_in.at[pl.ds(0, chips - 1), pl.ds(0, modes)], parts_recv)
+    total = parts_in[0, 0:modes]
+    for z in range(1, chips):
+        total = total + parts_in[z, 0:modes]
+    twice[pl.ds(gz, 1), 0:modes] = total.reshape(1, modes, quarter)
+    mine = twice.at[gz, pl.ds(0, modes)]
+    for target in peer_list:
+        send(mine, mine, twice_send, twice_recv, target)
+    for f in range(4):
+        facing = twice.at[4 * (1 + f + 1 - 2 * (f % 2)) + gz, pl.ds(0, modes)]
+        for k in range(nz):
+            send(mine, facing, twice_send, twice_recv, near(f, k))
+
+    await_bytes(twice.at[pl.ds(0, 4 * 5 - 1), pl.ds(0, modes)], twice_recv)
+
+    gather_wait(2)
+    curvature, cross = dot_totals(2, (2 * modes, 2 * modes + 1))
     step = resid_dot / curvature
-    next_dot = resid_dot - 2.0 * step * cross + step * step * square
-    ratio = next_dot / resid_dot
-    coeffs = [
-        [a - step * b for a, b in zip(first_coeffs[u], change_coeffs[u], strict=True)]
+    values = coarse_values(2)
+    image_coeffs = coefficients(values, 5)
+    less = [
+        [
+            across(
+                sum(
+                    fold(
+                        values[:, q * quarter : (q + 1) * quarter] * twice[4 * u + q, m : m + 1, :]
+                    )
+                    for q in range(nz)
+                )
+            )
+            for m in range(modes)
+        ]
         for u in range(5)
     ]
-    for f in range(4):
-        projected = scaled[:, face(f)] - step * change[:, face(f)] - correction(coeffs, f)
-        second[:, face(f)] = projected + ratio * direct[:, face(f)]
-    rows = product_a[...] - step * product_c[...] - corrected_product(coeffs)
-    rows = rows + ratio * product_b[...]
-    half = across(fold(second[:, block] * rows))
-    peers[pl.ds(gz, 1), :] = row_of([jnp.zeros((8, 1), f32)] * modes + [2.0 * half])
+    more = coefficients(coarse_values(2, modes), 5)
+    coeffs = [
+        [first_coeffs[u][m] - step * (more[u][m] - less[u][m]) for m in range(modes)]
+        for u in range(5)
+    ]
+    square = jnp.zeros((8, LANES), f32)
+    for f in range(4):
+        left = image[:, face(f)] - correction(image_coeffs, f)
+        right = weight[:, face(f)] * left
+        square = square + fold(left * right)
+        second[:, face(f)] = scaled[:, face(f)] - step * right - correction(coeffs, f)
+    square = across(square)
+    rows = product_c[...] - modes_times(op_heavy, image_coeffs)
+    rows = product_a[...] - step * rows - modes_times(op_modes, coeffs)
+    alone = across(fold(second[:, block] * rows))
+    mixed = across(fold(second[:, block] * product_b[...] + direct[:, block] * rows))
+    peers[pl.ds(gz, 1), :] = row_of([None] * modes + [2.0 * alone, 2.0 * mixed])
     mine = peers.at[pl.ds(gz, 1)]
     for target in peer_list:
         send(mine, mine, peer_send, peer_recv, target)
     await_bytes(peers.at[pl.ds(0, nz - 1)], peer_recv)
-    gather_start(4, jnp.sum(peers[...], axis=0, keepdims=True))
+    row = jnp.sum(peers[...], axis=0, keepdims=True) + row_of([None] * (modes + 2) + [square])
+    gather_start(3, row)
     for f in range(4):
         out_ref[:, face(f)] = out_ref[:, face(f)] + step * direct[:, face(f)]
-    gather_wait(4)
-    (curvature,) = dot_totals(4, (modes,))
-    step = next_dot / curvature
-    for f in range(4):
-        out_ref[:, face(f)] = out_ref[:, face(f)] + step * second[:, face(f)]
+    gather_wait(3)
+    alone, mixed, square = dot_totals(3, (modes, modes + 1, modes + 2))
+    next_dot = resid_dot - 2.0 * step * cross + step * step * square
+    ratio = next_dot / resid_dot
+    step = next_dot / (alone + ratio * mixed + ratio * ratio * curvature)
+    for f in range(4):
+        direction = second[:, face(f)] + ratio * direct[:, face(f)]
+        out_ref[:, face(f)] = out_ref[:, face(f)] + step * direction
 
     await_bytes(faces_out, faces_send)
     await_bytes(coarse.at[pl.ds(0, len(OFFSETS) - 1), pl.ds(0, modes)], coarse_send)
     await_bytes(plane.at[pl.ds(0, plane_size - 1)], plane_send)
     await_bytes(column.at[:, pl.ds(0, (chips - 1) * LANES)], column_send)
     await_bytes(peers.at[pl.ds(0, nz - 1)], peer_send)
-    await_bytes(pieces.at[pl.ds(0, 7)], piece_send)
     await_bytes(tiles_t.at[pl.ds(0, 7)], tile_send)
     for g in range(GATHERS):
         await_bytes(everyone.at[g, pl.ds(0, nx * ny - 1)], all_send.at[g])
+    await_bytes(chunks.at[pl.ds(0, chips - 1)], chunk_send)
+    await_bytes(plane_sc.at[pl.ds(0, plane_size - 1), pl.ds(0, modes)], sc_send)
+    await_bytes(parts_in.at[pl.ds(0, chips - 1), pl.ds(0, modes)], parts_send)
+    await_bytes(twice.at[pl.ds(0, 4 * 5 - 1), pl.ds(0, modes)], twice_send)
     for e in range(PRODUCTS):
         await_bytes(blocks.at[e, pl.ds(0, 7)], block_send.at[e])
 
@@ -588,6 +701,7 @@
         modes = traces.shape[2]
         cap = face_order.shape[3]
         padded = chips * LANES
+        quarter = padded // sizes[2]
         f32, i32 = jnp.float32, jnp.int32
         anywhere = pl.BlockSpec(memory_space=pl.ANY)
         vector = pltpu.VMEM((load_count, order), f32)
@@ -616,13 +730,17 @@
                 pltpu.VMEM((plane_size, LANES), f32),
                 pltpu.VMEM((8, padded), f32),
                 pltpu.VMEM((GATHERS, sizes[0] * sizes[1], LANES), f32),
-                pltpu.VMEM((8, padded), f32),
                 pltpu.VMEM((sizes[2], LANES), f32),
-                pltpu.VMEM((8, LANES), f32),
                 pltpu.VMEM((8, 40, LANES), f32),
                 pltpu.VMEM((5, 40, LANES), f32),
-                pltpu.VMEM((PRODUCTS, 8, 8, cap), f32),
+                pltpu.VMEM((PRODUCTS, 8, 16, cap // 2), jnp.bfloat16),
                 pltpu.VMEM((40, cap), f32),
+                pltpu.VMEM((40, cap), f32),
+                pltpu.VMEM((chips, 8, LANES), f32),
+                pltpu.VMEM((plane_size, 8, quarter), f32),
+                pltpu.VMEM((chips, 8, quarter), f32),
+                pltpu.VMEM((chips, 8, quarter), f32),
+                pltpu.VMEM((20, 8, quarter), f32),
                 pltpu.VMEM((8, order), i32),
                 pltpu.VMEM((8, order), i32),
             ]
@@ -631,8 +749,9 @@
             + [dma, dma((7,))]
             + [dma] * 8
             + [dma((GATHERS,))] * 2
-            + [dma] * 6
-            + [dma((PRODUCTS,))] * 2,
+            + [dma] * 4
+            + [dma((PRODUCTS,))] * 2
+            + [dma] * 8,
             compiler_params=pltpu.CompilerParams(
                 collective_id=0, has_side_effects=True, vmem_limit_bytes=60 << 20
             ),

time: 84.8 us -> 80.3 us (0.947)
  Pallas kernels: 82.4 us -> 78 us
    pallas_call x1, Pallas kernels: 82.4 us -> 78 us  [shards(): pl.pallas_call(functools.partial(kernel, sizes), out_shape=jax.ShapeDtype...]
where the time goes in v3:
time: 80.3 us; the launch traced here: 80.2 us
  Pallas kernels  78 us (97%)
  local copies, waits for them, and re-layouts  1.54 us (2%)
    pallas_call x1, Pallas kernels, shards(): pl.pallas_call(functools.partial(kernel, sizes), out_shape=jax.ShapeDtype...  78 us

profile of v3, /device:TPU:1, one launch (start us, length us, event | category | flops | bytes accessed | tf_op | source)
XLA Modules:
  0.0 80.2 jit_solution(11710524420934233057)
XLA Ops:
  0.7 78.0 %shard_map.91 = f32[8,3072]{1,0:T(8,128)} custom-call(bf16[768,3072]{1,0:T(8,128)(2,1)} %bitcast.9, f32[8,3072]{1,0:T(8,128)} %bitcast.11, f32[1,3072]{1,0:T(1,128)} %bitcast.14, f32[6,1,3072]{2,1,0:T(1,128)} %bitcast.12, f32[6,1,1152]{2,1,0:T(1,128)} %bitcast.13, f32[6,1,8]{2,1,0:T(1,128)} %bitcast.16, s32[1,4]{1,0:T(1,128)} %bitcast.17, ...), custom_call_target="tpu_custom_call" | custom-call | tf_op jit(solution)/shard_map/pallas_call | solution.py:714
  78.6 1.5 %copy.12 = f32[1,1,8,3072]{3,2,1,0:T(8,128)} copy(f32[1,1,8,3072]{3,2,1,0:T(8,128)} %bitcast.10) | data formatting | bytes 196608

commit v4 on v3

--- a/solution.py
+++ b/solution.py
@@ -40,12 +40,11 @@
     plane,
     column,
     everyone,
-    peers,
     tiles_t,
     mixing,
     blocks,
-    op_modes,
-    op_heavy,
+    all_modes,
+    all_heavy,
     chunks,
     plane_sc,
     parts_out,
@@ -63,9 +62,9 @@
     direct,
     second,
     change,
-    product_a,
-    product_b,
-    product_c,
+    all_a,
+    all_b,
+    all_c,
     op_sem,
     in_sem,
     faces_send,
@@ -78,8 +77,8 @@
     column_recv,
     all_send,
     all_recv,
-    peer_send,
-    peer_recv,
+    full_send,
+    full_recv,
     tile_send,
     tile_recv,
     block_send,
@@ -142,6 +141,8 @@
     def fetch(src, dst, sem):
         pltpu.make_async_copy(src, dst, sem).start()
 
+    op_modes, op_heavy = all_modes.at[gz], all_heavy.at[gz]
+
     barrier = pltpu.get_barrier_semaphore()
     greeted = (
         [shifted(dx, dy) for dx, dy in OFFSETS[1:]] + peer_list + plane_list + column_list + source_list
@@ -185,6 +186,14 @@
             send(mine, facing, send_sem, recv_sem, target)
         for target in peer_list:
             send(mine, mine, send_sem, recv_sem, target)
+
+    def to_peers(n, ref):
+        mine = ref.at[pl.ds(gz, 1)]
+        for target in peer_list:
+            send(mine, mine, full_send.at[n], full_recv.at[n], target)
+
+    def from_peers(n, ref):
+        await_bytes(ref.at[pl.ds(0, nz - 1)], full_recv.at[n])
 
     def take(values, index):
         return jnp.take_along_axis(values, index, axis=1, mode="promise_in_bounds")
@@ -509,6 +518,7 @@
         image[:, spot] = known[:, spot] - tile
 
     exchange_end(0, gap)
+    to_peers(0, all_modes)
 
     quarter = chips // nz * LANES
     share_of = pl.ds(pl.multiple_of(gz * quarter, LANES), quarter)
@@ -540,8 +550,10 @@
         sums[modes] = sums[modes] + fold(left * right)
     gather_start(1, row_of([across(x) for x in sums]))
 
-    product_a[...] = product(scaled)
+    all_a[pl.ds(gz, 1)] = product(scaled).reshape(1, 8, cap)
+    to_peers(1, all_a)
     modes_product(op_heavy, True)
+    to_peers(2, all_heavy)
 
     await_bytes(chunks.at[pl.ds(0, chips - 1)], chunk_recv)
     await_bytes(plane_sc.at[pl.ds(0, plane_size - 1), pl.ds(0, modes)], sc_recv)
@@ -569,9 +581,7 @@
 
     gather_wait(1)
     first_coeffs = coefficients(coarse_values(1), 5)
-    rows = product_a[...] - modes_times(op_modes, first_coeffs)
-    exchange_start(1, rows)
-    product_b[...] = rows
+    exchange_start(1, all_a[gz] - modes_times(op_modes, first_coeffs))
     (resid_dot,) = dot_totals(1, (modes,))
     for f in range(4):
         direct[:, face(f)] = scaled[:, face(f)] - correction(first_coeffs, f)
@@ -595,7 +605,8 @@
     for m in range(modes):
         sums[2 * modes + 1] = sums[2 * modes + 1] - 2.0 * sums[m] * first_coeffs[0][m]
     gather_start(2, row_of(sums))
-    product_c[...] = product(change)
+    all_c[pl.ds(gz, 1)] = product(change).reshape(1, 8, cap)
+    to_peers(3, all_c)
 
     await_bytes(parts_in.at[pl.ds(0, chips - 1), pl.ds(0, modes)], parts_recv)
     total = parts_in[0, 0:modes]
@@ -610,6 +621,12 @@
         for k in range(nz):
             send(mine, facing, twice_send, twice_recv, near(f, k))
 
+    from_peers(0, all_modes)
+    from_peers(1, all_a)
+    for k in range(nz):
+        all_b[k] = all_a[k] - modes_times(all_modes.at[k], first_coeffs)
+    from_peers(2, all_heavy)
+    from_peers(3, all_c)
     await_bytes(twice.at[pl.ds(0, 4 * 5 - 1), pl.ds(0, modes)], twice_recv)
 
     gather_wait(2)
@@ -643,16 +660,13 @@
         square = square + fold(left * right)
         second[:, face(f)] = scaled[:, face(f)] - step * right - correction(coeffs, f)
     square = across(square)
-    rows = product_c[...] - modes_times(op_heavy, image_coeffs)
-    rows = product_a[...] - step * rows - modes_times(op_modes, coeffs)
-    alone = across(fold(second[:, block] * rows))
-    mixed = across(fold(second[:, block] * product_b[...] + direct[:, block] * rows))
-    peers[pl.ds(gz, 1), :] = row_of([None] * modes + [2.0 * alone, 2.0 * mixed])
-    mine = peers.at[pl.ds(gz, 1)]
-    for target in peer_list:
-        send(mine, mine, peer_send, peer_recv, target)
-    await_bytes(peers.at[pl.ds(0, nz - 1)], peer_recv)
-    row = jnp.sum(peers[...], axis=0, keepdims=True) + row_of([None] * (modes + 2) + [square])
+    alone = mixed = jnp.zeros((8, LANES), f32)
+    for k in range(nz):
+        rows = all_c[k] - modes_times(all_heavy.at[k], image_coeffs)
+        rows = all_a[k] - step * rows - modes_times(all_modes.at[k], coeffs)
+        alone = alone + fold(second[:, face(k)] * rows)
+        mixed = mixed + fold(second[:, face(k)] * all_b[k] + direct[:, face(k)] * rows)
+    row = row_of([None] * modes + [2.0 * across(alone), 2.0 * across(mixed), square])
     gather_start(3, row)
     for f in range(4):
         out_ref[:, face(f)] = out_ref[:, face(f)] + step * direct[:, face(f)]
@@ -669,7 +683,8 @@
     await_bytes(coarse.at[pl.ds(0, len(OFFSETS) - 1), pl.ds(0, modes)], coarse_send)
     await_bytes(plane.at[pl.ds(0, plane_size - 1)], plane_send)
     await_bytes(column.at[:, pl.ds(0, (chips - 1) * LANES)], column_send)
-    await_bytes(peers.at[pl.ds(0, nz - 1)], peer_send)
+    for n, ref in enumerate((all_modes, all_a, all_heavy, all_c)):
+        await_bytes(ref.at[pl.ds(0, nz - 1)], full_send.at[n])
     await_bytes(tiles_t.at[pl.ds(0, 7)], tile_send)
     for g in range(GATHERS):
         await_bytes(everyone.at[g, pl.ds(0, nx * ny - 1)], all_send.at[g])
@@ -705,7 +720,7 @@
         f32, i32 = jnp.float32, jnp.int32
         anywhere = pl.BlockSpec(memory_space=pl.ANY)
         vector = pltpu.VMEM((load_count, order), f32)
-        block = pltpu.VMEM((load_count, cap), f32)
+        block = pltpu.VMEM((sizes[2], load_count, cap), f32)
         dma = pltpu.SemaphoreType.DMA
 
         def by_row(array):
@@ -713,7 +728,7 @@
 
         result = pl.pallas_call(
             functools.partial(kernel, sizes),
-            out_shape=jax.ShapeDtypeStruct((load_count, order), f32),
+            out_shape=pltpu.VMEM((load_count, order), f32),
             in_specs=[anywhere] * 9,
             out_specs=pl.BlockSpec(memory_space=pltpu.VMEM),
             scratch_shapes=[
@@ -730,12 +745,11 @@
                 pltpu.VMEM((plane_size, LANES), f32),
                 pltpu.VMEM((8, padded), f32),
                 pltpu.VMEM((GATHERS, sizes[0] * sizes[1], LANES), f32),
-                pltpu.VMEM((sizes[2], LANES), f32),
                 pltpu.VMEM((8, 40, LANES), f32),
                 pltpu.VMEM((5, 40, LANES), f32),
                 pltpu.VMEM((PRODUCTS, 8, 16, cap // 2), jnp.bfloat16),
-                pltpu.VMEM((40, cap), f32),
-                pltpu.VMEM((40, cap), f32),
+                pltpu.VMEM((sizes[2], 40, cap), f32),
+                pltpu.VMEM((sizes[2], 40, cap), f32),
                 pltpu.VMEM((chips, 8, LANES), f32),
                 pltpu.VMEM((plane_size, 8, quarter), f32),
                 pltpu.VMEM((chips, 8, quarter), f32),
@@ -749,7 +763,8 @@
             + [dma, dma((7,))]
             + [dma] * 8
             + [dma((GATHERS,))] * 2
-            + [dma] * 4
+            + [dma((4,))] * 2
+            + [dma] * 2
             + [dma((PRODUCTS,))] * 2
             + [dma] * 8,
             compiler_params=pltpu.CompilerParams(

time: 80.3 us -> 76.3 us (0.950)
  Pallas kernels: 78 us -> 74.8 us
  local copies, waits for them, and re-layouts: 1.54 us -> 0.64 us
    pallas_call x1, Pallas kernels: 78 us -> 74.8 us  [shards(): pl.pallas_call(functools.partial(kernel, sizes), out_shape=pltpu.VMEM((lo...]
    unnamed x1, local copies, waits for them, and re-layouts: 1.54 us -> 0.64 us
where the time goes in v4:
time: 76.3 us; the launch traced here: 76.2 us
  Pallas kernels  74.8 us (98%)
    pallas_call x1, Pallas kernels, shards(): pl.pallas_call(functools.partial(kernel, sizes), out_shape=pltpu.VMEM((lo...  74.8 us

profile of v4, /device:TPU:1, one launch (start us, length us, event | category | flops | bytes accessed | tf_op | source)
XLA Modules:
  0.0 76.2 jit_solution(14111724035267860882)
XLA Ops:
  0.7 74.8 %shard_map.91 = f32[8,3072]{1,0:T(8,128)S(1)} custom-call(bf16[768,3072]{1,0:T(8,128)(2,1)} %bitcast.10, f32[8,3072]{1,0:T(8,128)} %bitcast.11, f32[1,3072]{1,0:T(1,128)} %bitcast.14, f32[6,1,3072]{2,1,0:T(1,128)} %bitcast.12, f32[6,1,1152]{2,1,0:T(1,128)} %bitcast.13, f32[6,1,8]{2,1,0:T(1,128)} %bitcast.16, s32[1,4]{1,0:T(1,128)} %bitcast.17, ...), custom_call_target="tpu_custom_call" | custom-call | tf_op jit(solution)/shard_map/pallas_call | solution.py:729
  75.5 0.6 copy.11
